TPU v7x, 32 devices: a whole 2x2x4 slice. The times are simulated.
32 devices in a mesh: grp: 8 (over z, x), loc: 4 (over y, core).
Axes of the slice: x: 2, y: 2, z: 4, core: 2. Of those that a mesh axis runs over, the one named last changes fastest.
Arguments:
- tokens: bfloat16 [16384, 768], P(('grp', 'loc')), may hold values from -6 to 6
- cotangent: bfloat16 [16384, 768], P(('grp', 'loc')), may hold values from -6 to 6
- w_query: bfloat16 [768, 768], replicated, may hold values from -0.21875 to 0.21875
- w_key: bfloat16 [768, 768], replicated, may hold values from -0.21875 to 0.21875
- w_value: bfloat16 [768, 768], replicated, may hold values from -0.21875 to 0.21875
- w_output: bfloat16 [768, 768], replicated, may hold values from -1.75 to 1.75
- attn_gain: float32 [768], replicated, may hold values from 0.5 to 1.5
- bias_table: float32 [32, 12], replicated, may hold values from -4 to 4
- moe_gain: float32 [768], replicated, may hold values from 0.5 to 1.5
- router_weight: float32 [768, 32], replicated, may hold values from -0.25 to 0.25
- router_bias: float32 [32], replicated, may hold values from -0.75 to 0.75
- expert_in: bfloat16 [32, 768, 3072], P(('grp', 'loc')), may hold values from -0.21875 to 0.21875
- expert_out: bfloat16 [32, 3072, 768], P(('grp', 'loc')), may hold values from -6 to 6
- expert_ids: int32 [16384, 1], P(('grp', 'loc')), may hold values from 0 to 31; in each aligned block of 512 rows (0 to 511, 512 to 1023, ...) at most 32 rows name the same one
- bucket_ids: int32 [512, 512], replicated, may hold values from 0 to 31
Outputs:
- layer_out: bfloat16 [16384, 768], P(('grp', 'loc'))
- grad_tokens: bfloat16 [16384, 768], P(('grp', 'loc'))
- grad_query: float32 [768, 768], replicated
- grad_key: float32 [768, 768], replicated
- grad_value: float32 [768, 768], replicated
- grad_output: float32 [768, 768], replicated
- grad_attn_gain: float32 [768], replicated
- grad_table: float32 [32, 12], replicated
- grad_moe_gain: float32 [768], replicated
- grad_router: float32 [768, 32], replicated
- grad_router_bias: float32 [32], replicated
- grad_expert_in: float32 [32, 768, 3072], P(('grp', 'loc'))
- grad_expert_out: float32 [32, 3072, 768], P(('grp', 'loc'))
Inputs may be any that keep to these rules, and one draw needn't show every extreme that they name: `expert_ids`: in the rows of one device no expert is named by more than 32 rows, a bound that some block reaches of them.
All inputs are finite; a program needn't handle non-finite values.
Results may differ from a plain program's by a relative error of at most 0.018.
Values may be sent and summed in bfloat16 or wider, within the bound.
No kernel may reach another device: no remote copies, remote signals or barrier semaphores. Data moves between devices by JAX's collectives and lax.ppermute only.
A program may use at most 192 MiB of HBM per device.

v0:
```python
import functools

import jax
import jax.numpy as jnp
from jax import lax
from jax.experimental import pallas as pl
from jax.experimental.pallas import tpu as pltpu
from jax.sharding import PartitionSpec as P

AXES = ("grp", "loc")
LOW = jnp.bfloat16
F32 = jnp.float32
NN = (((1,), (0,)), ((), ()))
NT = (((1,), (1,)), ((), ()))
TN = (((0,), (0,)), ((), ()))
VMEM_BYTES = 56 * 1024 * 1024
EMPTY = 2.0**20


def dot(left, right, dims=NN):
    return lax.dot_general(left, right, dims, preferred_element_type=F32)


def split(values):
    high = values.astype(LOW)
    rest = values - high.astype(F32)
    middle = rest.astype(LOW)
    return high, middle, (rest - middle.astype(F32)).astype(LOW)


def params():
    return pltpu.CompilerParams(vmem_limit_bytes=VMEM_BYTES)


def cost(flops, nbytes, trans=0):
    return pl.CostEstimate(flops=int(flops), bytes_accessed=int(nbytes), transcendentals=int(trans))


def shape(dims, dtype):
    return jax.ShapeDtypeStruct(dims, dtype)


def norm_scale(values):
    return lax.rsqrt(jnp.mean(values * values, axis=-1, keepdims=True) + 1e-06)


def dispatch_kernel(ids_ref, dy_ref, out_ref, row_ref, col_ref, *, most):
    n = ids_ref.shape[1]
    slots = out_ref.shape[0]
    sub = lax.broadcasted_iota(jnp.int32, (n, n), 0)
    lane = lax.broadcasted_iota(jnp.int32, (n, n), 1)
    ids_row = ids_ref[...]
    ids_col = jnp.sum(jnp.where(sub == lane, ids_row, 0), axis=1, keepdims=True)
    same = ids_col == ids_row
    rank_row = jnp.sum(jnp.where(same & (sub < lane), 1, 0), axis=0, keepdims=True)
    rank_col = jnp.sum(jnp.where(same & (lane < sub), 1, 0), axis=1, keepdims=True)
    half = most // 2

    def halves(ids, rank):
        low = jnp.where(rank < half, ids * half + rank, -1)
        return low, jnp.where(rank < half, -1, ids * half + rank - half)

    low, high = halves(ids_row, rank_row)
    upper = lax.broadcasted_iota(jnp.int32, row_ref.shape, 0) < 4
    row_ref[...] = jnp.where(upper, low, high)
    low, high = halves(ids_col, rank_col)
    spot = lax.broadcasted_iota(jnp.int32, col_ref.shape, 1)
    full = ids_col * most + rank_col
    col_ref[...] = jnp.where(spot < 32, low, jnp.where(spot < 64, high, full))
    place = lax.broadcasted_iota(jnp.int32, (slots, n), 0) == ids_row * most + rank_row
    hot = place.astype(F32)
    filled = jnp.sum(hot, axis=1, keepdims=True)
    rows = dot(hot.astype(LOW), dy_ref[...])
    out_ref[...] = jnp.where(filled > 0.0, rows, EMPTY).astype(LOW)


def dispatch(ids, dy, slots, most):
    n, width = dy.shape
    return pl.pallas_call(
        functools.partial(dispatch_kernel, most=most),
        out_shape=(
            shape((slots, width), LOW),
            shape((8, n), jnp.int32),
            shape((n, 128), jnp.int32),
        ),
        compiler_params=params(),
        cost_estimate=cost(2 * slots * n * width, 4 * slots * width),
        name="dispatch",
    )(ids.reshape(1, n), dy)


def attend_kernel(
    tok_ref,
    gain_ref,
    tab_ref,
    bucket_ref,
    wq_ref,
    wk_ref,
    wv_ref,
    wo_ref,
    moe_gain_ref,
    row_ref,
    q_ref,
    k_ref,
    v_ref,
    w_ref,
    att_t_ref,
    normed_t_ref,
    mid_ref,
    low_ref,
    high_ref,
    wt_ref,
    att_s,
    normed_s,
    *,
    scaling,
):
    step = pl.program_id(0)
    pairs = pl.num_programs(0)
    n = tok_ref.shape[0]

    @pl.when(step == 0)
    def _():
        inputs = tok_ref[...].astype(F32)
        normed_one = (inputs * norm_scale(inputs) * gain_ref[...]).astype(LOW)
        normed_s[...] = normed_one
        normed_t_ref[...] = normed_one.T

    normed = normed_s[...]
    query = dot(normed, wq_ref[...]).astype(LOW)
    keys = dot(normed, wk_ref[...]).astype(LOW)
    values = dot(normed, wv_ref[...]).astype(LOW)
    q_ref[...] = query
    k_ref[...] = keys
    v_ref[...] = values
    span = query.shape[1]
    for i, ref in enumerate((wq_ref, wk_ref, wv_ref)):
        wt_ref[i * span : (i + 1) * span, :] = ref[...].T
    low_half = lax.broadcasted_iota(jnp.int32, query.shape, 1) < query.shape[1] // 2
    zero = jnp.zeros_like(query)
    total = jnp.zeros((n, query.shape[1]), F32)
    for h in range(2):
        mine = low_half if h == 0 else ~low_half
        scores = dot(jnp.where(mine, query, zero), keys, NT) * scaling
        table = jnp.broadcast_to(tab_ref[step, pl.ds(h, 1), :], (n, 128))
        bias = [
            jnp.take_along_axis(
                table, bucket_ref[:, c * 128 : (c + 1) * 128], axis=1, mode="promise_in_bounds"
            )
            for c in range(n // 128)
        ]
        scores = scores + jnp.concatenate(bias, axis=1)
        top = jnp.max(scores, axis=1, keepdims=True)
        grown = jnp.exp(scores - top)
        weights = (grown * (1.0 / jnp.sum(grown, axis=1, keepdims=True))).astype(LOW)
        w_ref[h] = weights
        total = total + dot(weights, jnp.where(mine, values, zero))
    att_s[step] = total.astype(LOW)

    @pl.when(step == pairs - 1)
    def _():
        attended = jnp.concatenate([att_s[i] for i in range(att_s.shape[0])], axis=1)
        att_t_ref[...] = attended.T
        middle = tok_ref[...].astype(F32) + dot(attended, wo_ref[...])
        mid_ref[...] = middle
        normed_two = (middle * norm_scale(middle) * moe_gain_ref[...]).astype(LOW)
        for ref, row in ((low_ref, 0), (high_ref, 4)):
            slot = lax.broadcasted_iota(jnp.int32, (ref.shape[0], n), 0)
            place = slot == row_ref[row : row + 1, :]
            ref[...] = dot(place.astype(F32).astype(LOW), normed_two).astype(LOW)


def attend(tokens, gain, table, buckets, wq, wk, wv, wo, moe_gain, row, slots, n_heads):
    n, width = tokens.shape
    pairs = n_heads // 2
    span = width // pairs
    whole = lambda *dims: pl.BlockSpec(dims, lambda p: (0,) * len(dims))
    cols = lambda rows: pl.BlockSpec((rows, span), lambda p: (0, p))
    return pl.pallas_call(
        functools.partial(attend_kernel, scaling=(width // n_heads) ** -0.5),
        grid=(pairs,),
        in_specs=[
            whole(n, width),
            whole(1, width),
            whole(*table.shape),
            whole(n, n),
            cols(width),
            cols(width),
            cols(width),
            whole(width, width),
            whole(1, width),
            whole(8, n),
        ],
        out_specs=[
            cols(n),
            cols(n),
            cols(n),
            pl.BlockSpec((2, n, n), lambda p: (p, 0, 0)),
            whole(width, n),
            whole(width, n),
            whole(n, width),
            whole(slots // 2, width),
            whole(slots // 2, width),
            pl.BlockSpec((3 * span, width), lambda p: (p, 0)),
        ],
        out_shape=[
            shape((n, width), LOW),
            shape((n, width), LOW),
            shape((n, width), LOW),
            shape((n_heads, n, n), LOW),
            shape((width, n), LOW),
            shape((width, n), LOW),
            shape((n, width), F32),
            shape((slots // 2, width), LOW),
            shape((slots // 2, width), LOW),
            shape((3 * width, width), LOW),
        ],
        scratch_shapes=[pltpu.VMEM((pairs, n, span), LOW), pltpu.VMEM((n, width), LOW)],
        compiler_params=params(),
        cost_estimate=cost(
            8 * n * width * width + 4 * n_heads * n * n * span + 2 * slots * n * width,
            2 * n_heads * n * n + 24 * n * width,
            n_heads * n * n,
        ),
        name="attend",
    )(
        tokens,
        gain.reshape(1, width),
        table,
        buckets,
        wq,
        wk,
        wv,
        wo,
        moe_gain.reshape(1, width),
        row,
    )


def arrive_kernel(dy_ref, low_ref, high_ref, low_kept, high_kept, *, most, keep):
    slots = dy_ref.shape[0]
    half = most // 2
    edge = dy_ref[:, 0:128]
    valid = jnp.where(edge.astype(F32) < EMPTY * 0.5, 1.0, 0.0).astype(LOW)
    sub = lax.broadcasted_iota(jnp.int32, (slots, slots), 0)
    lane = lax.broadcasted_iota(jnp.int32, (slots, slots), 1)
    before = jnp.where(lane < sub, 1.0, 0.0).astype(LOW)
    first = jnp.where(lax.broadcasted_iota(jnp.int32, (8, 128), 1) == 0, 1.0, 0.0).astype(LOW)
    valid_row = dot(first, valid, NT)
    slot_row = dot(valid_row.astype(LOW), before, NT)
    kept = ((valid_row > 0.5) & (slot_row < keep - 0.5))[0:1, :]
    sub = lax.broadcasted_iota(jnp.int32, (slots // 2, slots), 0)
    lane = lax.broadcasted_iota(jnp.int32, (slots // 2, slots), 1)
    here = sub // half * most + sub % half
    for at, ref, kept_ref in ((0, low_ref, low_kept), (half, high_ref, high_kept)):
        place = jnp.where((lane == here + at) & kept, 1.0, 0.0)
        kept_ref[...] = jnp.broadcast_to(jnp.sum(place, axis=1, keepdims=True), kept_ref.shape)
        ref[...] = dot(place.astype(LOW), dy_ref[...]).astype(LOW)


def arrive(dy_rows, most, keep):
    slots, width = dy_rows.shape
    return pl.pallas_call(
        functools.partial(arrive_kernel, most=most, keep=keep),
        out_shape=(
            shape((slots // 2, width), LOW),
            shape((slots // 2, width), LOW),
            shape((slots // 2, 128), F32),
            shape((slots // 2, 128), F32),
        ),
        compiler_params=params(),
        cost_estimate=cost(2 * slots * slots * width, 4 * slots * width),
        name="arrive",
    )(dy_rows)


def expert_kernel(
    me_ref, x_ref, dyc_ref, kept_ref, router_ref, rbias_ref, win_ref, wout_ref, *refs, n_in
):
    dn_ref, res_ref, hid_ref, dpre_ref, dres_ref, dlog_ref, sum_s, drow_s, prob_s = refs[n_in:]
    step = pl.program_id(0)

    def gate_of(probs):
        mine = lax.broadcasted_iota(jnp.int32, probs.shape, 1) == me_ref[0]
        return mine, jnp.sum(jnp.where(mine, probs, 0.0), axis=1, keepdims=True)

    @pl.when(step == 0)
    def _():
        rows = x_ref[...]
        high, middle, low = split(router_ref[...])
        logits = dot(rows, high) + (dot(rows, middle) + dot(rows, low)) + rbias_ref[...]
        grown = jnp.exp(logits - jnp.max(logits, axis=1, keepdims=True))
        probs = grown / jnp.sum(grown, axis=1, keepdims=True)
        prob_s[...] = probs
        dres_ref[...] = (gate_of(probs)[1] * dyc_ref[...].astype(F32)).astype(LOW)
        sum_s[...] = jnp.zeros_like(sum_s)
        drow_s[...] = jnp.zeros_like(drow_s)

    rows = x_ref[...]
    win = win_ref[...]
    wout = wout_ref[...]
    pre = dot(rows, win)
    rate = 0.7978845608028654
    square = pre * pre
    tanh = jnp.tanh(rate * pre * (1.0 + 0.044715 * square))
    half = 0.5 * (1.0 + tanh)
    hidden = (pre * half).astype(LOW)
    slope = half + (0.5 * rate) * pre * (1.0 - tanh * tanh) * (1.0 + 3 * 0.044715 * square)
    dhid = dot(dres_ref[...], wout, NT)
    dpre = (dhid * slope).astype(LOW)
    hid_ref[...] = hidden
    dpre_ref[...] = dpre
    sum_s[...] += dot(hidden, wout)
    drow_s[...] += dot(dpre, win, NT)

    @pl.when(step == pl.num_programs(0) - 1)
    def _():
        result = sum_s[...].astype(LOW).astype(F32)
        dgate = jnp.sum(dyc_ref[...].astype(F32) * result, axis=1, keepdims=True)
        probs = prob_s[...]
        mine, gate = gate_of(probs)
        dlogits = probs * (jnp.where(mine, dgate, 0.0) - gate * dgate)
        dlog_ref[...] = dlogits
        high, middle, _ = split(router_ref[...])
        dhigh, dmiddle, _ = split(dlogits)
        side = dot(dhigh, high, NT) + (dot(dhigh, middle, NT) + dot(dmiddle, high, NT))
        dn_ref[...] = (drow_s[...] + side).astype(LOW)
        res_ref[...] = (kept_ref[:, 0:1] * gate * result).astype(LOW)


def expert(me, rows, dyc, kept, router, rbias, expert_in, expert_out, earlier=()):
    n, width = rows.shape
    n_exp = router.shape[1]
    ff = expert_in.shape[2]
    block = 768 if ff % 768 == 0 else ff
    at = 1 if earlier else 0
    whole = lambda *dims: pl.BlockSpec(dims, lambda f: (0,) * len(dims))
    return pl.pallas_call(
        functools.partial(expert_kernel, n_in=len(earlier)),
        grid=(ff // block,),
        in_specs=[
            pl.BlockSpec(memory_space=pltpu.SMEM),
            whole(n, width),
            whole(n, width),
            whole(n, 128),
            whole(width, n_exp),
            whole(1, n_exp),
            pl.BlockSpec((None, width, block), lambda f: (0, 0, f)),
            pl.BlockSpec((None, block, width), lambda f: (0, f, 0)),
        ]
        + [pl.BlockSpec(memory_space=pl.ANY)] * len(earlier),
        out_specs=[
            whole(n, width),
            whole(n, width),
            pl.BlockSpec((n, block), lambda f: (at, f)),
            pl.BlockSpec((n, block), lambda f: (at, f)),
            pl.BlockSpec((n, width), lambda f: (at, 0)),
            pl.BlockSpec((n, n_exp), lambda f: (at, 0)),
        ],
        out_shape=[
            shape((n, width), LOW),
            shape((n, width), LOW),
            shape((2 * n, ff), LOW),
            shape((2 * n, ff), LOW),
            shape((2 * n, width), LOW),
            shape((2 * n, n_exp), F32),
        ],
        scratch_shapes=[
            pltpu.VMEM((n, width), F32),
            pltpu.VMEM((n, width), F32),
            pltpu.VMEM((n, n_exp), F32),
        ],
        input_output_aliases={8 + i: 2 + i for i in range(len(earlier))},
        compiler_params=params(),
        cost_estimate=cost(8 * n * width * ff, 16 * width * ff, n * ff),
        name="expert",
    )(me, rows, dyc, kept, router, rbias.reshape(1, n_exp), expert_in, expert_out, *earlier)


def weights_kernel(
    low_ref, high_ref, hid_ref, dpre_ref, dres_ref, dlog_ref, in_ref, out_ref, routed_ref, bias_ref,
    x_s,
):
    @pl.when(pl.program_id(0) == 0)
    def _():
        n = low_ref.shape[0]
        x_s[:, :n] = low_ref[...].T
        x_s[:, n:] = high_ref[...].T
        dlogits = dlog_ref[...]
        rows = x_s[...]
        high, middle, low = split(dlogits)
        routed = dot(rows, high) + (dot(rows, middle) + dot(rows, low))
        routed_ref[...] = jnp.zeros_like(routed_ref)
        routed_ref[:, : routed.shape[1]] = routed
        bias_ref[...] = jnp.broadcast_to(jnp.sum(dlogits, axis=0, keepdims=True), bias_ref.shape)

    in_ref[...] = dot(x_s[...], dpre_ref[...])
    out_ref[...] = dot(hid_ref[...].T, dres_ref[...])


def weights_back(x_low, x_high, hidden, dpre, dres, dlogits):
    n, width = x_low.shape
    ff = hidden.shape[1]
    n_exp = dlogits.shape[1]
    tail = -(-n_exp // 128) * 128
    block = 512 if ff % 512 == 0 else ff
    whole = lambda *dims: pl.BlockSpec(dims, lambda f: (0,) * len(dims))
    cols = lambda rows: pl.BlockSpec((rows, block), lambda f: (0, f))
    return pl.pallas_call(
        weights_kernel,
        grid=(ff // block,),
        in_specs=[
            whole(n, width),
            whole(n, width),
            cols(2 * n),
            cols(2 * n),
            whole(2 * n, width),
            whole(2 * n, n_exp),
        ],
        out_specs=[
            cols(width),
            pl.BlockSpec((block, width), lambda f: (f, 0)),
            whole(width, tail),
            whole(8, n_exp),
        ],
        out_shape=[
            shape((width, ff), F32),
            shape((ff, width), F32),
            shape((width, tail), F32),
            shape((8, n_exp), F32),
        ],
        scratch_shapes=[pltpu.VMEM((width, 2 * n), LOW)],
        compiler_params=params(),
        cost_estimate=cost(8 * n * width * ff, 8 * width * ff),
        name="weights_back",
    )(x_low, x_high, hidden, dpre, dres, dlogits)


def back_kernel(
    core_ref,
    low_hbm,
    high_hbm,
    col_hbm,
    mid_hbm,
    dy_hbm,
    wo_hbm,
    attended_hbm,
    routed_hbm,
    normed_hbm,
    gain_ref,
    q_ref,
    k_ref,
    v_ref,
    w_ref,
    dmid_hbm,
    sent_hbm,
    kept_hbm,
    gain_out,
    grads_ref,
    ds_ref,
    sent_b,
    kept_b,
    datt_s,
    low_ref,
    high_ref,
    col_ref,
    mid_ref,
    dy_ref,
    wo_ref,
    attended_ref,
    routed_ref,
    normed_ref,
    dmid_ref,
    sent_a,
    kept_a,
    sems,
    *,
    scaling,
):
    step = pl.program_id(0)
    n, span = q_ref.shape
    width = mid_ref.shape[1]
    part = width // 2
    half = span // 2
    tail = routed_ref.shape[1]
    lead = sent_a.shape[1] - tail - width
    lead_pairs = lead // (3 * span)
    sides = [
        pl.ds(pl.multiple_of(core * part, 128), part) for core in (1 - core_ref[0], core_ref[0])
    ]
    ins = [
        (low_hbm, low_ref),
        (high_hbm, high_ref),
        (col_hbm, col_ref),
        (mid_hbm, mid_ref),
        (dy_hbm, dy_ref),
        (wo_hbm, wo_ref),
        (attended_hbm, attended_ref),
        (routed_hbm, routed_ref),
        (normed_hbm, normed_ref),
    ]
    outs = [(dmid_ref, dmid_hbm), (sent_a, sent_hbm), (kept_a, kept_hbm)]
    copies = [
        pltpu.make_async_copy(source, target, sems.at[at])
        for at, (source, target) in enumerate(ins + outs)
    ]
    from_low, from_high, from_col, from_mid, from_dy, from_wo, from_att, from_routed = copies[:8]
    from_normed, to_dmid, to_sent, to_kept = copies[8:]

    @pl.when(step == 0)
    def _():
        for copy in copies[:9]:
            copy.start()
        dnormed = jnp.zeros((n, width), F32)
        from_col.wait()
        for copy, ref, at in ((from_low, low_ref, 0), (from_high, high_ref, 32)):
            place = lax.broadcasted_iota(jnp.int32, (n, ref.shape[0]), 1) == col_ref[:, at : at + 1]
            copy.wait()
            dnormed = dnormed + dot(place.astype(F32).astype(LOW), ref[...])
        from_mid.wait()
        from_dy.wait()
        middle = mid_ref[...]
        inv = norm_scale(middle)
        scaled = dnormed * gain_ref[...]
        inner = jnp.mean(scaled * middle, axis=1, keepdims=True)
        dmid = dy_ref[...].astype(F32) + inv * scaled - middle * (inv * inv * inv) * inner
        dmid_ref[...] = dmid
        to_dmid.start()
        branch = dmid.astype(LOW)
        from_wo.wait()
        datt = dot(branch, wo_ref[...], NT).astype(LOW)
        for p in range(datt_s.shape[0]):
            datt_s[p] = datt[:, p * span : (p + 1) * span]
        gain_out[...] = jnp.broadcast_to(
            jnp.sum(dnormed * middle * inv, axis=0, keepdims=True), gain_out.shape
        )
        from_att.wait()
        from_routed.wait()
        for ref, rows in zip((sent_a, kept_a), sides):
            ref[:, :width] = dot(attended_ref[rows, :], branch).astype(LOW)
            ref[:, width + lead :] = routed_ref[rows, :].astype(LOW)
        from_normed.wait()

    @pl.when(step > 0)
    def _():
        pair = step - 1
        query, keys, values, grad = q_ref[...], k_ref[...], v_ref[...], datt_s[pair]
        low_half = lax.broadcasted_iota(jnp.int32, query.shape, 1) < half
        low_rows = lax.broadcasted_iota(jnp.int32, (span, n), 0) < half

        def stack(value):
            zero = jnp.zeros_like(value)
            return jnp.concatenate(
                [jnp.where(low_half, value, zero), jnp.where(low_half, zero, value)], axis=0
            )

        def spread(value):
            value = value.astype(F32).T.astype(LOW)
            zero = jnp.zeros_like(value)
            return jnp.concatenate(
                [jnp.where(low_rows, value, zero), jnp.where(low_rows, zero, value)], axis=1
            )

        weights_low = jnp.concatenate([w_ref[0], w_ref[1]], axis=0)
        weights = weights_low.astype(F32)
        both = weights * dot(stack(grad), values, NT)
        dscores = (both - weights * jnp.sum(both, axis=1, keepdims=True)).astype(LOW)
        ds_ref[0] = dscores[:n]
        ds_ref[1] = dscores[n:]
        dquery = dot(jnp.concatenate([dscores[:n], dscores[n:]], axis=1), stack(keys))
        dvalues = dot(spread(grad), weights_low)
        dkeys = dot(spread(query), dscores)
        grads = jnp.concatenate([dquery * scaling, dkeys.T * scaling, dvalues.T], axis=1)
        grads = grads.astype(LOW)
        grads_ref[...] = grads
        products = [dot(normed_ref[rows, :], grads).astype(LOW) for rows in sides]

        @pl.when(pair < lead_pairs)
        def _():
            at = pl.multiple_of(width + pair * (3 * span), 128)
            for ref, product in zip((sent_a, kept_a), products):
                ref[:, pl.ds(at, 3 * span)] = product

        @pl.when(pair >= lead_pairs)
        def _():
            for ref, product in zip((sent_b, kept_b), products):
                ref[...] = product

    @pl.when(step == lead_pairs)
    def _():
        to_sent.start()
        to_kept.start()

    @pl.when(step == pl.num_programs(0) - 1)
    def _():
        to_dmid.wait()
        to_sent.wait()
        to_kept.wait()


def back(
    core, low, high, col, middle, dy, moe_gain, wo, attended_t, routed, query, keys, values, weights,
    normed_t, lead_pairs,
):
    n_heads, n, _ = weights.shape
    width = low.shape[1]
    pairs = n_heads // 2
    span = width // pairs
    part = width // 2
    columns_a = width + 3 * span * lead_pairs + routed.shape[1]
    columns_b = 3 * span * (pairs - lead_pairs)
    pair = lambda p: jnp.maximum(p - 1, 0)
    late = lambda p: jnp.maximum(p - 1 - lead_pairs, 0)
    cols = lambda size: pl.BlockSpec((n, size), lambda p: (0, pair(p)))
    square = pl.BlockSpec((2, n, n), lambda p: (pair(p), 0, 0))
    piece = pl.BlockSpec((part, 3 * span), lambda p: (0, late(p)))
    anywhere = pl.BlockSpec(memory_space=pl.ANY)
    loaded = (low, high, col, middle, dy, wo, attended_t, routed, normed_t)
    return pl.pallas_call(
        functools.partial(back_kernel, scaling=(width // n_heads) ** -0.5),
        grid=(1 + pairs,),
        in_specs=[pl.BlockSpec(memory_space=pltpu.SMEM)]
        + [anywhere] * len(loaded)
        + [pl.BlockSpec((1, width), lambda p: (0, 0)), cols(span), cols(span), cols(span), square],
        out_specs=[anywhere] * 3
        + [pl.BlockSpec((8, width), lambda p: (0, 0)), cols(3 * span), square, piece, piece],
        out_shape=[
            shape((n, width), F32),
            shape((part, columns_a), LOW),
            shape((part, columns_a), LOW),
            shape((8, width), F32),
            shape((n, 3 * width), LOW),
            shape((n_heads, n, n), LOW),
            shape((part, columns_b), LOW),
            shape((part, columns_b), LOW),
        ],
        scratch_shapes=[pltpu.VMEM((pairs, n, span), LOW)]
        + [pltpu.VMEM(value.shape, value.dtype) for value in loaded]
        + [
            pltpu.VMEM((n, width), F32),
            pltpu.VMEM((part, columns_a), LOW),
            pltpu.VMEM((part, columns_a), LOW),
            pltpu.SemaphoreType.DMA((len(loaded) + 3,)),
        ],
        compiler_params=params(),
        cost_estimate=cost(1000, 1000),
        name="back",
    )(core, *loaded, moe_gain.reshape(1, width), query, keys, values, weights)


def table_kernel(ds_ref, bucket_ref, out_ref, sum_s, *, n_buckets):
    step = pl.program_id(0)
    n_heads, rows, n = ds_ref.shape
    band = 16

    @pl.when(step == 0)
    def _():
        sum_s[...] = jnp.zeros_like(sum_s)

    total = sum_s[...]
    for r in range(rows // band):
        span = slice(r * band, (r + 1) * band)
        grads = ds_ref[:, span, :].reshape(n_heads * band, n)
        buckets = bucket_ref[span, :]
        hot = jnp.concatenate(
            [jnp.where(buckets == b, 1.0, 0.0).astype(LOW) for b in range(n_buckets)], axis=0
        )
        total = total + dot(grads, hot, NT)
    sum_s[...] = total

    @pl.when(step == pl.num_programs(0) - 1)
    def _():
        left = lax.broadcasted_iota(jnp.int32, total.shape, 0) % band
        right = lax.broadcasted_iota(jnp.int32, total.shape, 1) % band
        own = jnp.where(left == right, total, 0.0)
        own = jnp.sum(own.reshape(n_heads, band, n_buckets * band), axis=1)
        bucket = lax.broadcasted_iota(jnp.int32, (n_buckets * band, n_buckets), 1)
        column = lax.broadcasted_iota(jnp.int32, (n_buckets * band, n_buckets), 0)
        fold = jnp.where(column // band == bucket, 1.0, 0.0).astype(LOW)
        high, middle, low = split(own)
        out_ref[...] = dot(high, fold) + dot(middle, fold) + dot(low, fold)


def table_back(dscores, buckets, n_buckets):
    n_heads, n, _ = dscores.shape
    rows, band = 64, 16
    dims = (n_heads * band, n_buckets * band)
    return pl.pallas_call(
        functools.partial(table_kernel, n_buckets=n_buckets),
        grid=(n // rows,),
        in_specs=[
            pl.BlockSpec((n_heads, rows, n), lambda r: (0, r, 0)),
            pl.BlockSpec((rows, n), lambda r: (r, 0)),
        ],
        out_specs=pl.BlockSpec((n_heads, n_buckets), lambda r: (0, 0)),
        out_shape=shape((n_heads, n_buckets), F32),
        scratch_shapes=[pltpu.VMEM(dims, F32)],
        compiler_params=params(),
        cost_estimate=cost(2 * dims[0] * dims[1] * n * n // band, 2 * n_heads * n * n),
        name="table_back",
    )(dscores, buckets)


def add(left, right):
    return (left.astype(F32) + right.astype(F32)).astype(LOW)


def tie(*values):
    return lax.optimization_barrier(values)


class Ring:
    def __init__(self, n_grp, n_loc):
        size = n_grp * n_loc
        bits = size.bit_length() - 1
        low = n_loc.bit_length() - 1
        self.size = size
        ys, xs = list(range(1, low)), list(range(low, bits - 2))
        first, second = (ys + xs, xs + ys) if len(ys) == len(xs) else (ys + xs, ys + xs)
        self.plane = list(zip(first, second))
        self.near, self.far = (bits - 2, bits - 2), (bits - 1, bits - 1)
        self.core = (0, 0)

    def swap(self, value, shifts):
        pairs = [(i, i ^ (1 << shifts[i & 1])) for i in range(self.size)]
        return lax.ppermute(value, AXES, pairs)

    def side(self, me, shifts):
        shift = jnp.where(me & 1 == 0, shifts[0], shifts[1])
        return (me >> shift) & 1

    def cut(self, value, me, shifts):
        halves = value.reshape(2, value.shape[0] // 2, value.shape[1])
        side = self.side(me, shifts)
        return [lax.dynamic_index_in_dim(halves, at, 0, keepdims=False) for at in (1 - side, side)]

    def join(self, value, got, me, shifts):
        side = self.side(me, shifts)
        low = jnp.where(side == 0, value, got)
        high = jnp.where(side == 0, got, value)
        return jnp.concatenate([low, high], axis=0)

    def where(self, me):
        sides = [self.side(me, self.plane[0]), self.side(me ^ 1, self.plane[0])]
        return jnp.stack([me & 1] + sides)


def unpack_kernel(where_ref, own_a, core_a, own_b, core_b, *refs):
    mine = pl.program_id(0) == where_ref[0]
    rows_a = jnp.where(mine, own_a[...], core_a[...]).astype(F32)
    rows_b = jnp.where(mine, own_b[...], core_b[...]).astype(F32)
    outs = refs[-5:]
    width = outs[3].shape[1]
    outs[3][...] = rows_a[:, :width]
    span = 128
    half = rows_b.shape[1] // 3
    rest = width + 3 * half
    outs[4][...] = rows_a[:, rest : rest + outs[4].shape[1]]
    for i in range(3):
        for p in range(half // span):
            at = (3 * p + i) * span
            here = slice(p * span, (p + 1) * span)
            outs[i][:, here] = rows_a[:, width + at : width + at + span]
            there = slice(half + p * span, half + (p + 1) * span)
            outs[i][:, there] = rows_b[:, at : at + span]


def unpack(where, own_a, core_a, own_b, core_b, late, earlier, width, n_experts):
    rows = own_a.shape[0]
    parts = 1
    size = rows // parts
    earlier = tuple(earlier)

    def place(c, r, where_ref):
        side = jnp.where(c == where_ref[0], where_ref[1], where_ref[2])
        return (2 * c + (1 - side if late else side)) * parts + r, 0

    piece = lambda value: pl.BlockSpec((size, value.shape[1]), lambda c, r, where_ref: (r, 0))
    return pl.pallas_call(
        unpack_kernel,
        grid_spec=pltpu.PrefetchScalarGridSpec(
            num_scalar_prefetch=1,
            grid=(2, parts),
            in_specs=[piece(value) for value in (own_a, core_a, own_b, core_b)]
            + [pl.BlockSpec(memory_space=pl.ANY)] * len(earlier),
            out_specs=[pl.BlockSpec((size, width), place)] * 4
            + [pl.BlockSpec((size, n_experts), place)],
        ),
        out_shape=[shape((width, width), F32)] * 4 + [shape((width, n_experts), F32)],
        input_output_aliases={5 + i: i for i in range(len(earlier))},
        compiler_params=params(),
        cost_estimate=cost(rows * width, 24 * rows * width),
        name="unpack",
    )(where, own_a, core_a, own_b, core_b, *earlier)


def tokens_kernel(grads_ref, wt_ref, tok_ref, gain_ref, dmid_ref, out_ref, gain_out, sum_s):
    step = pl.program_id(0)
    part = dot(grads_ref[...], wt_ref[...])

    @pl.when(step == 0)
    def _():
        sum_s[...] = part

    @pl.when(step > 0)
    def _():
        sum_s[...] += part

    @pl.when(step == pl.num_programs(0) - 1)
    def _():
        dnormed = sum_s[...]
        inputs = tok_ref[...].astype(F32)
        inv = norm_scale(inputs)
        scaled = dnormed * gain_ref[...]
        inner = jnp.mean(scaled * inputs, axis=1, keepdims=True)
        out_ref[...] = (
            dmid_ref[...] + inv * scaled - inputs * (inv * inv * inv) * inner
        ).astype(LOW)
        gain_out[...] = jnp.broadcast_to(
            jnp.sum(dnormed * inputs * inv, axis=0, keepdims=True), gain_out.shape
        )


def tokens_back(grads, weights_t, tokens, gain, dmid):
    n, width = tokens.shape
    steps = 3
    block = grads.shape[1] // steps
    whole = lambda *dims: pl.BlockSpec(dims, lambda p: (0,) * len(dims))
    return pl.pallas_call(
        tokens_kernel,
        grid=(steps,),
        in_specs=[
            pl.BlockSpec((n, block), lambda p: (0, p)),
            pl.BlockSpec((block, width), lambda p: (p, 0)),
            whole(n, width),
            whole(1, width),
            whole(n, width),
        ],
        out_specs=[whole(n, width), whole(8, width)],
        out_shape=[shape((n, width), LOW), shape((8, width), F32)],
        scratch_shapes=[pltpu.VMEM((n, width), F32)],
        compiler_params=params(),
        cost_estimate=cost(6 * n * width * width, 6 * width * width + 14 * n * width),
        name="tokens_back",
    )(grads, weights_t, tokens, gain.reshape(1, width), dmid)


def leave_kernel(res_ref, col_ref, mid_ref, out_ref):
    n = mid_ref.shape[0]
    slots = res_ref.shape[0]
    place = lax.broadcasted_iota(jnp.int32, (n, slots), 1) == col_ref[:, 64:65]
    out_ref[...] = (mid_ref[...] + dot(place.astype(F32).astype(LOW), res_ref[...])).astype(LOW)


def leave(res_rows, col, middle):
    n, width = middle.shape
    return pl.pallas_call(
        leave_kernel,
        out_shape=shape((n, width), LOW),
        compiler_params=params(),
        cost_estimate=cost(2 * n * width * res_rows.shape[0], 10 * n * width),
        name="leave",
    )(res_rows, col, middle)


def exchange(rows):
    return lax.all_to_all(rows, AXES, split_axis=0, concat_axis=0, tiled=True)


def sum_small(parts, n_dev):
    flat = jnp.concatenate([part.reshape(-1) for part in parts])
    size = flat.shape[0]
    lines = -(-size // 1024) * 8
    block = jnp.pad(flat, (0, lines * 128 - size)).reshape(1, lines, 128)
    sent = jnp.broadcast_to(block, (n_dev, lines, 128))
    total = jnp.sum(exchange(sent), axis=0).reshape(-1)
    found, start = [], 0
    for part in parts:
        found.append(total[start : start + part.size].reshape(part.shape))
        start += part.size
    return found


def body(
    n_grp,
    n_loc,
    tokens,
    cotangent,
    w_query,
    w_key,
    w_value,
    w_output,
    attn_gain,
    bias_table,
    moe_gain,
    router_weight,
    router_bias,
    expert_in,
    expert_out,
    expert_ids,
    bucket_ids,
):
    n_rows, width = tokens.shape
    n_buckets, n_heads = bias_table.shape
    n_experts = router_weight.shape[1]
    most = max(2, 2 * n_rows // n_experts)
    slots = n_experts * most
    keep = 5 * n_rows // 4
    me = (lax.axis_index("grp") * lax.axis_size("loc") + lax.axis_index("loc")).reshape(1)

    dy_out, row, col = dispatch(expert_ids, cotangent, slots, most)
    dy_out, attn_gain, moe_gain, bias_table = tie(dy_out, attn_gain, moe_gain, bias_table)
    dy_rows = exchange(dy_out)

    table = jnp.pad(bias_table.T, ((0, 0), (0, 128 - n_buckets))).reshape(n_heads // 2, 2, 128)
    query, keys, values, weights, attended_t, normed_t, middle, x_low, x_high, weights_t = attend(
        tokens, attn_gain, table, bucket_ids, w_query, w_key, w_value, w_output, moe_gain, row,
        slots, n_heads,
    )
    dy_rows, x_low = tie(dy_rows, x_low)
    x_low = exchange(x_low)
    arrived = arrive(dy_rows, most, keep)
    x_low, x_high, *arrived = tie(x_low, x_high, *arrived)
    dy_low, dy_high, kept_low, kept_high = arrived
    x_high = exchange(x_high)
    model = (router_weight, router_bias, expert_in, expert_out)
    dn_low, res_low, *earlier = expert(me, x_low, dy_low, kept_low, *model)
    dn_low, x_high = tie(dn_low, x_high)
    dn_low = exchange(dn_low)
    from_high = expert(me, x_high, dy_high, kept_high, *model, earlier)
    dn_low, *from_high = tie(dn_low, *from_high)
    dn_high, res_high, hidden, dpre, dres, dlogits = from_high
    dn_high = exchange(dn_high)
    res_sent = jnp.concatenate(
        [value.reshape(n_experts, most // 2, width) for value in (res_low, res_high)], axis=1
    ).reshape(slots, width)
    grad_expert_in, grad_expert_out, routed, bias_rows = weights_back(
        x_low, x_high, hidden, dpre, dres, dlogits
    )
    grad_router_bias = bias_rows[0]
    ring = Ring(n_grp, n_loc)
    rank = me[0]
    where = ring.where(rank)
    dn_high, res_sent, grad_expert_in, grad_expert_out, routed, grad_router_bias, where = tie(
        dn_high, res_sent, grad_expert_in, grad_expert_out, routed, grad_router_bias, where
    )
    res_rows = exchange(res_sent)
    dmid, sent_a, kept_a, moe_gain_rows, grads, dscores, sent_b, kept_b = back(
        me & 1, dn_low, dn_high, col, middle, cotangent, moe_gain, w_output, attended_t, routed, query,
        keys, values, weights, normed_t, n_heads // 4,
    )

    def step(kept, got, shifts):
        kept, got = ring.cut(kept, rank, shifts), ring.cut(got, rank, shifts)
        return [add(left, right) for left, right in zip(kept, got)]

    got_a = ring.swap(sent_a, ring.core)
    sent_a, kept_a = step(kept_a, got_a, ring.plane[0])
    got_b = ring.swap(sent_b, ring.core)
    got_b, sent_a = tie(got_b, sent_a)
    got_a = ring.swap(sent_a, ring.plane[0])
    sent_b, kept_b = step(kept_b, got_b, ring.plane[0])
    sent_b, grads = tie(sent_b, grads)
    got_b = ring.swap(sent_b, ring.plane[0])
    grad_tokens, attn_gain_rows = tokens_back(grads, weights_t, tokens, attn_gain, dmid)
    got_a, got_b, grad_tokens, attn_gain_rows, res_rows = tie(
        got_a, got_b, grad_tokens, attn_gain_rows, res_rows
    )
    for shifts in ring.plane[1:] + [ring.near]:
        sent_a, kept_a = step(kept_a, got_a, shifts)
        sent_b, kept_b = step(kept_b, got_b, shifts)
        got_a, got_b = ring.swap(sent_a, shifts), ring.swap(sent_b, shifts)
    value_a, value_b = add(kept_a, got_a), add(kept_b, got_b)
    value_a, value_b, dscores = tie(value_a, value_b, dscores)
    got_a, got_b = ring.swap(value_a, ring.far), ring.swap(value_b, ring.far)
    grad_table = table_back(dscores, bucket_ids, n_buckets)
    got_a, got_b, grad_table = tie(got_a, got_b, grad_table)
    value_a, value_b = add(value_a, got_a), add(value_b, got_b)
    for place, shifts in enumerate(reversed(ring.plane[1:] + [ring.near])):
        if place == 0:
            value_a, value_b, res_rows = tie(value_a, value_b, res_rows)
        if place == 1:
            value_a, value_b, grad_table = tie(value_a, value_b, grad_table)
        got_a, got_b = ring.swap(value_a, shifts), ring.swap(value_b, shifts)
        if place == 0:
            layer_out = leave(res_rows, col, middle)
            got_a, got_b, layer_out = tie(got_a, got_b, layer_out)
        if place == 1:
            smalls = sum_small(
                (attn_gain_rows[0], grad_table, moe_gain_rows[0], grad_router_bias), n_grp * n_loc
            )
        value_a = ring.join(value_a, got_a, rank, shifts)
        value_b = ring.join(value_b, got_b, rank, shifts)
    near_a, near_b = ring.swap(value_a, ring.plane[0]), ring.swap(value_b, ring.plane[0])
    core_a, core_b = ring.swap(value_a, ring.core), ring.swap(value_b, ring.core)
    outs = unpack(where, value_a, core_a, value_b, core_b, False, (), width, n_experts)
    near_a, near_b, *rest = tie(near_a, near_b, *outs, *smalls)
    outs, smalls = rest[:5], rest[5:]
    far_a, far_b = ring.swap(near_a, ring.core), ring.swap(near_b, ring.core)
    outs = unpack(where, near_a, far_a, near_b, far_b, True, outs, width, n_experts)
    grad_query, grad_key, grad_value, grad_output, grad_router = outs
    grad_attn_gain, grad_table, grad_moe_gain, grad_router_bias = smalls
    return (
        layer_out,
        grad_tokens,
        grad_query,
        grad_key,
        grad_value,
        grad_output,
        grad_attn_gain,
        grad_table.T,
        grad_moe_gain,
        grad_router,
        grad_router_bias,
        grad_expert_in[None],
        grad_expert_out[None],
    )


def solution(mesh):
    rows, flat = P(AXES, None), P(AXES, None, None)
    return jax.shard_map(
        functools.partial(body, mesh.shape["grp"], mesh.shape["loc"]),
        mesh=mesh,
        in_specs=(
            rows, rows, P(), P(), P(), P(), P(), P(), P(), P(), P(), flat, flat, rows, P(),
        ),
        out_specs=(
            rows, rows, P(), P(), P(), P(), P(), P(), P(), P(), P(), flat, flat,
        ),
        check_vma=False,
    )
```

profile of v0, /device:TPU:0, one launch (start us, length us, event | category | flops | bytes accessed | tf_op | source)
XLA Modules:
  0.0 281.4 jit_solution(6689598441636874971)
XLA Ops:
  0.6 3.8 %dispatch.1 = (bf16[1024,768]{1,0:T(8,128)(2,1)}, s32[8,512]{1,0:T(8,128)}, s32[512,128]{1,0:T(8,128)}) custom-call(s32[1,512]{1,0:T(1,128)} %bitcast.97, bf16[512,768]{1,0:T(8,128)(2,1)} %dy_hbm.1), custom_call_target="tpu_custom_call" | custom-call | flops 805306368 | bytes 3145728 | tf_op jit(solution)/shard_map/dispatch/pallas_call | solution.py:79
  4.5 7.3 %all-to-all-start = ((bf16[32,32,768]{2,1,0:T(8,128)(2,1)}), bf16[32,32,768]{2,1,0:T(8,128)(2,1)S(1)}, u32[]{:S(2)}, u32[]{:S(2)}) async-start(bf16[32,32,768]{2,1,0:T(8,128)(2,1)} %bitcast.76), calls=%async_computation | async-start | bytes 3145728 | tf_op jit(solution)/shard_map/all_to_all | solution.py:867
  13.6 26.2 %attend.1 = (bf16[512,768]{1,0:T(8,128)(2,1)}, bf16[512,768]{1,0:T(8,128)(2,1)}, bf16[512,768]{1,0:T(8,128)(2,1)}, bf16[12,512,512]{2,1,0:T(8,128)(2,1)}, bf16[7...) custom-call(bf16[512,768]{1,0:T(8,128)(2,1)} %tok_ref.3, ...), custom_call_target="tpu_custom_call" | custom-call | flops 4831838208 | bytes 15728640 | tf_op jit(solution)/shard_map/attend/pallas_call | solution.py:179
  39.8 9.5 %all-to-all-done = bf16[32,32,768]{2,1,0:T(8,128)(2,1)S(1)} async-done(((bf16[32,32,768]{2,1,0:T(8,128)(2,1)}), bf16[32,32,768]{2,1,0:T(8,128)(2,1)S(1)}, u32[]{:S(2)}, u32[]{:S(2)}) %all-to-all-start) | async-done | bytes 1572896 | tf_op jit(solution)/shard_map/all_to_all | solution.py:867
  49.3 3.7 %all-to-all-start.1 = ((bf16[32,16,768]{2,1,0:T(8,128)(2,1)}), bf16[32,16,768]{2,1,0:T(8,128)(2,1)S(1)}, u32[]{:S(2)}, u32[]{:S(2)}) async-start(bf16[32,16,768]{2,1,0:T(8,128)(2,1)} %bitcast.87), calls=%async_computation.1 | async-start | bytes 1572864 | tf_op jit(solution)/shard_map/all_to_all | solution.py:867
  53.0 5.2 %arrive.1 = (bf16[512,768]{1,0:T(8,128)(2,1)}, bf16[512,768]{1,0:T(8,128)(2,1)}, f32[512,128]{1,0:T(8,128)}, f32[512,128]{1,0:T(8,128)}) custom-call(bf16[1024,768]{1,0:T(8,128)(2,1)} %bitcast.75), custom_call_target="tpu_custom_call" | custom-call | flops 1610612736 | bytes 3145728 | tf_op jit(solution)/shard_map/arrive/pallas_call | solution.py:263
  58.2 15.4 %all-to-all-done.1 = bf16[32,16,768]{2,1,0:T(8,128)(2,1)S(1)} async-done(((bf16[32,16,768]{2,1,0:T(8,128)(2,1)}), bf16[32,16,768]{2,1,0:T(8,128)(2,1)S(1)}, u32[]{:S(2)}, u32[]{:S(2)}) %all-to-all-start.1) | async-done | bytes 786464 | tf_op jit(solution)/shard_map/all_to_all | solution.py:867
  73.6 3.8 %all-to-all-start.2 = ((bf16[32,16,768]{2,1,0:T(8,128)(2,1)}), bf16[32,16,768]{2,1,0:T(8,128)(2,1)S(1)}, u32[]{:S(2)}, u32[]{:S(2)}) async-start(bf16[32,16,768]{2,1,0:T(8,128)(2,1)} %bitcast.8), calls=%async_computation.2 | async-start | bytes 1572864 | tf_op jit(solution)/shard_map/all_to_all | solution.py:867
  78.4 18.0 %expert.2 = (bf16[512,768]{1,0:T(8,128)(2,1)}, bf16[512,768]{1,0:T(8,128)(2,1)}, bf16[1024,3072]{1,0:T(8,128)(2,1)}, bf16[1024,3072]{1,0:T(8,128)(2,1)}, bf16[1024,768]{1,0:T(8,128)(2,1)}, /*index=5*/f32[1024,32]{1,0:T(8,128)}) custom-call(s32[1]{0:T(128)} %bitcast.me_ref, bf16[512,768]{1,0:T(8,128)(2,1)} %bitcast.82, ...), custom_call_target="tpu_custom_call" | custom-call | flops 9663676416 | bytes 37748736 | tf_op jit(solution)/shard_map/expert/pallas_call | solution.py:338
  96.3 1.5 all-to-all-done.2
  97.9 4.2 %all-to-all-start.3 = ((bf16[32,16,768]{2,1,0:T(8,128)(2,1)}), bf16[32,16,768]{2,1,0:T(8,128)(2,1)S(1)}, u32[]{:S(2)}, u32[]{:S(2)}) async-start(bf16[32,16,768]{2,1,0:T(8,128)(2,1)} %bitcast.88), calls=%async_computation.3 | async-start | bytes 1572864 | tf_op jit(solution)/shard_map/all_to_all | solution.py:867
  102.1 18.0 %expert.3 = (bf16[512,768]{1,0:T(8,128)(2,1)}, bf16[512,768]{1,0:T(8,128)(2,1)}, bf16[1024,3072]{1,0:T(8,128)(2,1)}, bf16[1024,3072]{1,0:T(8,128)(2,1)}, bf16[1024,768]{1,0:T(8,128)(2,1)}, /*index=5*/f32[1024,32]{1,0:T(8,128)}) custom-call(s32[1]{0:T(128)} %bitcast.me_ref, ...), custom_call_target="tpu_custom_call", output_to_operand_aliasing={{2}: (8, {}), {3}: (9, {}), {4}: (10, {}), {5}: (11, {})} | custom-call | flops 9663676416 | bytes 37748736 | tf_op jit(solution)/shard_map/expert/pallas_call | solution.py:338
  120.1 2.6 all-to-all-done.3
  122.7 3.6 %all-to-all-start.4 = ((bf16[32,16,768]{2,1,0:T(8,128)(2,1)}), bf16[32,16,768]{2,1,0:T(8,128)(2,1)S(1)}, u32[]{:S(2)}, u32[]{:S(2)}) async-start(bf16[32,16,768]{2,1,0:T(8,128)(2,1)} %bitcast.86), calls=%async_computation.4 | async-start | bytes 1572864 | tf_op jit(solution)/shard_map/all_to_all | solution.py:867
  126.9 1.4 pad_maximum_fusion
  128.3 16.8 %weights_back.1 = (f32[768,3072]{1,0:T(8,128)}, f32[3072,768]{1,0:T(8,128)}, f32[768,128]{1,0:T(8,128)}, f32[8,32]{1,0:T(8,128)}) custom-call(bf16[512,768]{1,0:T(8,128)(2,1)} %bitcast.83, bf16[512,768]{1,0:T(8,128)(2,1)} %bitcast.85, bf16[1024,3072]{1,0:T(8,128)(2,1)} %get-tuple-element.166.hid_ref, bf16[1024,3072]{1,0:T(8,128)(2,1)} %get-tuple-element.167.dpre_ref, ...), custom_call_target="tpu_custom_call" | custom-call | flops 9663676416 | bytes 18874368 | tf_op jit(solution)/shard_map/weights_back/pallas_call | solution.py:409
  147.9 4.9 %all-to-all-start.5 = ((bf16[32,32,768]{2,1,0:T(8,128)(2,1)}), bf16[32,32,768]{2,1,0:T(8,128)(2,1)S(1)}, u32[]{:S(2)}, u32[]{:S(2)}) async-start(bf16[32,32,768]{2,1,0:T(8,128)(2,1)} %bitcast.28), calls=%async_computation.5 | async-start | bytes 3145728 | tf_op jit(solution)/shard_map/all_to_all | solution.py:867
  152.8 20.4 %back.1 = (f32[512,768]{1,0:T(8,128)}, bf16[384,2048]{1,0:T(8,128)(2,1)}, bf16[384,2048]{1,0:T(8,128)(2,1)}, f32[8,768]{1,0:T(8,128)}, bf16[512,2304]{1,0:T(8,12...) custom-call(s32[1]{0:T(128)S(6)} %and.16.core_ref, ...), custom_call_target="tpu_custom_call" | custom-call | flops 1000 | bytes 1000 | tf_op jit(solution)/shard_map/back/pallas_call | solution.py:619
  173.8 4.4 %collective-permute-done = bf16[384,2048]{1,0:T(8,128)(2,1)S(1)} collective-permute-done((bf16[384,2048]{1,0:T(8,128)(2,1)}, bf16[384,2048]{1,0:T(8,128)(2,1)S(1)}, u32[]{:S(2)}, u32[]{:S(2)}) %collective-permute-start) | collective-permute-done | bytes 1572896 | tf_op jit(solution)/shard_map/ppermute | solution.py:726
  179.4 3.4 %add_convert_fusion.1 = (bf16[1,192,2048]{2,1,0:T(8,128)(2,1)S(1)}, bf16[192,2048]{1,0:T(8,128)(2,1)}) fusion(bf16[2,192,2048]{2,1,0:T(8,128)(2,1)} %bitcast.74, s32[]{:T(128)S(6)} %select_n.117, bf16[2,192,2048]{2,1,0:T(8,128)(2,1)} %bitcast.73, s32[]{:T(128)S(6)} %select_n.120), kind=kLoop, calls=%fused_computation.2 | loop fusion | flops 3145728 | bytes 4718600 | tf_op jit(solution)/shard_map/convert_element_type | solution.py:705
  183.9 2.1 add_convert_fusion.2
  187.0 7.2 %tokens_back.1 = (bf16[512,768]{1,0:T(8,128)(2,1)}, f32[8,768]{1,0:T(8,128)}) custom-call(bf16[512,2304]{1,0:T(8,128)(2,1)} %get-tuple-element.192.grads_ref, bf16[2304,768]{1,0:T(8,128)(2,1)} %get-tuple-element.193.wt_ref, bf16[512,768]{1,0:T(8,128)(2,1)} %tok_ref.3, f32[1,768]{1,0:T(1,128)} %reshape.173.gain_ref, f32[512,768]{1,0:T(8,128)} %get-tuple-element.194.dmid_ref), custom_call_target="tpu_custom_call" | custom-call | flops 1811939328 | bytes 9043968 | tf_op jit(solution)/shard_map/tokens_back/pallas_call | solution.py:829
  194.2 6.2 %collective-permute-done.3 = bf16[192,1152]{1,0:T(8,128)(2,1)S(1)} collective-permute-done((bf16[192,1152]{1,0:T(8,128)(2,1)}, bf16[192,1152]{1,0:T(8,128)(2,1)S(1)}, u32[]{:S(2)}, u32[]{:S(2)}) %collective-permute-start.3) | collective-permute-done | bytes 442400 | tf_op jit(solution)/shard_map/ppermute | solution.py:726
  201.4 1.5 collective-permute-start.6
  202.8 1.4 add_convert_fusion.5
  204.8 2.8 collective-permute-done.6
  208.5 2.1 collective-permute-start.7
  210.6 1.5 collective-permute-done.4
  212.1 2.1 collective-permute-start.5
  215.2 2.7 collective-permute-done.5
  217.9 1.6 collective-permute-start.8
  219.5 1.4 collective-permute-start.9
  220.9 10.0 %table_back.1 = f32[12,32]{1,0:T(8,128)} custom-call(bf16[12,512,512]{2,1,0:T(8,128)(2,1)} %get-tuple-element.203.ds_ref, s32[512,512]{1,0:T(8,128)} %bucket_ref.3), custom_call_target="tpu_custom_call" | custom-call | flops 3221225472 | bytes 6291456 | tf_op jit(solution)/shard_map/table_back/pallas_call | solution.py:688
  230.9 1.2 collective-permute-done.9
  233.1 1.2 collective-permute-start.11
  234.3 4.0 %leave.1 = bf16[512,768]{1,0:T(8,128)(2,1)} custom-call(bf16[1024,768]{1,0:T(8,128)(2,1)} %bitcast.68, s32[512,128]{1,0:T(8,128)} %get-tuple-element.175.col_hbm.col_ref, f32[512,768]{1,0:T(8,128)} %get-tuple-element.176.mid_hbm.mid_ref), custom_call_target="tpu_custom_call" | custom-call | flops 805306368 | bytes 3932160 | tf_op jit(solution)/shard_map/leave/pallas_call | solution.py:857
  238.2 1.7 collective-permute-done.11
  240.1 1.5 collective-permute-start.12
  243.9 4.9 %all-to-all-start.6 = ((f32[32,16,128]{2,1,0:T(8,128)}), f32[32,16,128]{2,1,0:T(8,128)S(1)}, u32[]{:S(2)}, u32[]{:S(2)}) async-start(f32[32,16,128]{2,1,0:T(8,128)} %broadcast_in_dim.14), calls=%async_computation.6 | async-start | bytes 524288 | tf_op jit(solution)/shard_map/all_to_all | solution.py:867
  248.9 1.8 collective-permute-start.14
  250.9 1.5 collective-permute-start.13
  252.4 6.2 %collective-permute-done.14 = bf16[96,1152]{1,0:T(8,128)(2,1)S(1)} collective-permute-done((bf16[96,1152]{1,0:T(8,128)(2,1)S(1)}, bf16[96,1152]{1,0:T(8,128)(2,1)S(1)}, u32[]{:S(2)}, u32[]{:S(2)}) %collective-permute-start.14) | collective-permute-done | bytes 221216 | tf_op jit(solution)/shard_map/ppermute | solution.py:726
  258.8 1.7 collective-permute-start.15
  263.3 4.7 %unpack.2 = (f32[768,768]{1,0:T(8,128)}, f32[768,768]{1,0:T(8,128)}, f32[768,768]{1,0:T(8,128)}, f32[768,768]{1,0:T(8,128)}, f32[768,32]{1,0:T(8,128)}) custom-call(s32[3]{0:T(128)} %pad_add_fusion.where_ref, bf16[192,2048]{1,0:T(8,128)(2,1)} %copy-done.3, bf16[192,2048]{1,0:T(8,128)(2,1)} %copy-done.13, bf16[192,1152]{1,0:T(8,128)(2,1)} %copy-done.4, ...), custom_call_target="tpu_custom_call" | custom-call | flops 147456 | bytes 3538944 | tf_op jit(solution)/shard_map/unpack/pallas_call | solution.py:779
  268.0 2.2 collective-permute-done.15.own_b
  270.7 2.6 collective-permute-done.19.core_b
  275.0 4.7 %unpack.3 = (f32[768,768]{1,0:T(8,128)}, f32[768,768]{1,0:T(8,128)}, f32[768,768]{1,0:T(8,128)}, f32[768,768]{1,0:T(8,128)}, f32[768,32]{1,0:T(8,128)}) custom-call(s32[3]{0:T(128)} %pad_add_fusion.where_ref, bf16[192,2048]{1,0:T(8,128)(2,1)} %copy-done.8, ...), custom_call_target="tpu_custom_call", output_to_operand_aliasing={{0}: (5, {}), {1}: (6, {}), {2}: (7, {}), {3}: (8, {}), {4}... | custom-call | flops 147456 | bytes 3538944 | tf_op jit(solution)/shard_map/unpack/pallas_call | solution.py:779
  279.6 1.8 copy.42
  (97 shorter events, 22.1 us)
Async XLA Ops:
  4.5 7.3 %copy-start.19 = (f32[768]{0:T(1024)S(1)}, f32[768]{0:T(1024)}, u32[]{:S(2)}) copy-start(f32[768]{0:T(1024)} %param.21) | copy-start | bytes 9220
  4.5 7.9 %copy-start.20 = (f32[768]{0:T(1024)S(1)}, f32[768]{0:T(1024)}, u32[]{:S(2)}) copy-start(f32[768]{0:T(1024)} %param.23) | copy-start | bytes 9220
  4.5 8.5 %copy-start.18 = (f32[32,12]{0,1:T(8,128)S(1)}, f32[32,12]{0,1:T(8,128)}, u32[]{:S(2)}) copy-start(f32[32,12]{0,1:T(8,128)} %param.22) | copy-start | bytes 4612
  4.5 44.8 %all-to-all-start = ((bf16[32,32,768]{2,1,0:T(8,128)(2,1)}), bf16[32,32,768]{2,1,0:T(8,128)(2,1)S(1)}, u32[]{:S(2)}, u32[]{:S(2)}) async-start(bf16[32,32,768]{2,1,0:T(8,128)(2,1)} %bitcast.76), calls=%async_computation | async-start | bytes 3145728 | tf_op jit(solution)/shard_map/all_to_all | solution.py:867
  49.3 3.7 %copy-start.6 = (bf16[32,32,768]{2,1,0:T(8,128)(2,1)}, bf16[32,32,768]{2,1,0:T(8,128)(2,1)S(1)}, u32[]{:S(2)}) copy-start(bf16[32,32,768]{2,1,0:T(8,128)(2,1)S(1)} %all-to-all-done) | copy-start | bytes 4718596
  49.3 24.3 %all-to-all-start.1 = ((bf16[32,16,768]{2,1,0:T(8,128)(2,1)}), bf16[32,16,768]{2,1,0:T(8,128)(2,1)S(1)}, u32[]{:S(2)}, u32[]{:S(2)}) async-start(bf16[32,16,768]{2,1,0:T(8,128)(2,1)} %bitcast.87), calls=%async_computation.1 | async-start | bytes 1572864 | tf_op jit(solution)/shard_map/all_to_all | solution.py:867
  58.2 19.2 %copy-start.16 = (f32[768,32]{0,1:T(8,128)S(1)}, f32[768,32]{0,1:T(8,128)}, u32[]{:S(2)}) copy-start(f32[768,32]{0,1:T(8,128)} %param.24) | copy-start | bytes 294916
  73.6 4.8 %copy-start.10 = (bf16[32,16,768]{2,1,0:T(8,128)(2,1)}, bf16[32,16,768]{2,1,0:T(8,128)(2,1)S(1)}, u32[]{:S(2)}) copy-start(bf16[32,16,768]{2,1,0:T(8,128)(2,1)S(1)} %all-to-all-done.1) | copy-start | bytes 2359300
  73.6 24.2 %all-to-all-start.2 = ((bf16[32,16,768]{2,1,0:T(8,128)(2,1)}), bf16[32,16,768]{2,1,0:T(8,128)(2,1)S(1)}, u32[]{:S(2)}, u32[]{:S(2)}) async-start(bf16[32,16,768]{2,1,0:T(8,128)(2,1)} %bitcast.8), calls=%async_computation.2 | async-start | bytes 1572864 | tf_op jit(solution)/shard_map/all_to_all | solution.py:867
  97.9 4.2 %copy-start.11 = (bf16[32,16,768]{2,1,0:T(8,128)(2,1)}, bf16[32,16,768]{2,1,0:T(8,128)(2,1)S(1)}, u32[]{:S(2)}) copy-start(bf16[32,16,768]{2,1,0:T(8,128)(2,1)S(1)} %all-to-all-done.2) | copy-start | bytes 2359300
  97.9 24.8 %all-to-all-start.3 = ((bf16[32,16,768]{2,1,0:T(8,128)(2,1)}), bf16[32,16,768]{2,1,0:T(8,128)(2,1)S(1)}, u32[]{:S(2)}, u32[]{:S(2)}) async-start(bf16[32,16,768]{2,1,0:T(8,128)(2,1)} %bitcast.88), calls=%async_computation.3 | async-start | bytes 1572864 | tf_op jit(solution)/shard_map/all_to_all | solution.py:867
  120.1 6.8 %copy-start.12 = (bf16[512,768]{1,0:T(8,128)(2,1)S(1)}, bf16[512,768]{1,0:T(8,128)(2,1)}, u32[]{:S(2)}) copy-start(bf16[512,768]{1,0:T(8,128)(2,1)} %get-tuple-element.164) | copy-start | bytes 2359300
  120.1 6.8 %copy-start.14 = (bf16[512,768]{1,0:T(8,128)(2,1)S(1)}, bf16[512,768]{1,0:T(8,128)(2,1)}, u32[]{:S(2)}) copy-start(bf16[512,768]{1,0:T(8,128)(2,1)} %get-tuple-element.165) | copy-start | bytes 2359300
  122.7 5.6 %copy-start.1 = (bf16[32,16,768]{2,1,0:T(8,128)(2,1)}, bf16[32,16,768]{2,1,0:T(8,128)(2,1)S(1)}, u32[]{:S(2)}) copy-start(bf16[32,16,768]{2,1,0:T(8,128)(2,1)S(1)} %all-to-all-done.3) | copy-start | bytes 2359300
  122.7 24.2 %all-to-all-start.4 = ((bf16[32,16,768]{2,1,0:T(8,128)(2,1)}), bf16[32,16,768]{2,1,0:T(8,128)(2,1)S(1)}, u32[]{:S(2)}, u32[]{:S(2)}) async-start(bf16[32,16,768]{2,1,0:T(8,128)(2,1)} %bitcast.86), calls=%async_computation.4 | async-start | bytes 1572864 | tf_op jit(solution)/shard_map/all_to_all | solution.py:867
  146.9 0.9 copy-start.2
  147.9 52.6 %all-to-all-start.5 = ((bf16[32,32,768]{2,1,0:T(8,128)(2,1)}), bf16[32,32,768]{2,1,0:T(8,128)(2,1)S(1)}, u32[]{:S(2)}, u32[]{:S(2)}) async-start(bf16[32,32,768]{2,1,0:T(8,128)(2,1)} %bitcast.28), calls=%async_computation.5 | async-start | bytes 3145728 | tf_op jit(solution)/shard_map/all_to_all | solution.py:867
  173.2 5.0 %collective-permute-start = (bf16[384,2048]{1,0:T(8,128)(2,1)}, bf16[384,2048]{1,0:T(8,128)(2,1)S(1)}, u32[]{:S(2)}, u32[]{:S(2)}) collective-permute-start(bf16[384,2048]{1,0:T(8,128)(2,1)} %get-tuple-element.185), channel_id=1, source_target_pairs={{0,1},{1,0},{2,3},{3,2},{4,5},{5,4},{6,7},{7,6},{8,9},{9,8},{10,11... | collective-permute-start | bytes 4718600 | tf_op jit(solution)/shard_map/ppermute | solution.py:726
  173.3 9.4 %collective-permute-start.1 = (bf16[384,1152]{1,0:T(8,128)(2,1)}, bf16[384,1152]{1,0:T(8,128)(2,1)}, u32[]{:S(2)}, u32[]{:S(2)}) collective-permute-start(bf16[384,1152]{1,0:T(8,128)(2,1)} %get-tuple-element.186), channel_id=1, source_target_pairs={{0,1},{1,0},{2,3},{3,2},{4,5},{5,4},{6,7},{7,6},{8,9},{9,8},{10,11... | collective-permute-start | bytes 2654216 | tf_op jit(solution)/shard_map/ppermute | solution.py:726
  178.2 1.2 copy-start.5
  179.3 4.6 %copy-start.7 = (bf16[384,1152]{1,0:T(8,128)(2,1)S(1)}, bf16[384,1152]{1,0:T(8,128)(2,1)}, u32[]{:S(2)}) copy-start(bf16[384,1152]{1,0:T(8,128)(2,1)} %get-tuple-element.188) | copy-start | bytes 2654212
  182.8 17.6 %collective-permute-start.2 = (bf16[192,2048]{1,0:T(8,128)(2,1)}, bf16[192,2048]{1,0:T(8,128)(2,1)}, u32[]{:S(2)}, u32[]{:S(2)}) collective-permute-start(bf16[192,2048]{1,0:T(8,128)(2,1)} %get-tuple-element.187), channel_id=1, source_target_pairs={{0,2},{1,5},{2,0},{3,7},{4,6},{5,1},{6,4},{7,3},{8,10},{9,13},{10,... | collective-permute-start | bytes 2359304 | tf_op jit(solution)/shard_map/ppermute | solution.py:726
  186.1 14.3 %collective-permute-start.3 = (bf16[192,1152]{1,0:T(8,128)(2,1)}, bf16[192,1152]{1,0:T(8,128)(2,1)S(1)}, u32[]{:S(2)}, u32[]{:S(2)}) collective-permute-start(bf16[192,1152]{1,0:T(8,128)(2,1)} %get-tuple-element.191), channel_id=1, source_target_pairs={{0,2},{1,5},{2,0},{3,7},{4,6},{5,1},{6,4},{7,3},{8,10},{9,13},{10,... | collective-permute-start | bytes 1327112 | tf_op jit(solution)/shard_map/ppermute | solution.py:726
  200.4 3.8 %copy-start = (bf16[32,32,768]{2,1,0:T(8,128)(2,1)}, bf16[32,32,768]{2,1,0:T(8,128)(2,1)S(1)}, u32[]{:S(2)}) copy-start(bf16[32,32,768]{2,1,0:T(8,128)(2,1)S(1)} %all-to-all-done.5) | copy-start | bytes 4718596
  201.4 6.2 %collective-permute-start.6 = (bf16[96,1152]{1,0:T(8,128)(2,1)}, bf16[96,1152]{1,0:T(8,128)(2,1)}, u32[]{:S(2)}, u32[]{:S(2)}) collective-permute-start(bf16[96,1152]{1,0:T(8,128)(2,1)} %get-tuple-element.278), channel_id=1, source_target_pairs={{0,4},{1,3},{2,6},{3,1},{4,0},{5,7},{6,2},{7,5},{8,12},{9,11},{10,... | collective-permute-start | bytes 663560 | tf_op jit(solution)/shard_map/ppermute | solution.py:726
  204.2 7.8 %collective-permute-start.4 = (bf16[96,2048]{1,0:T(8,128)(2,1)S(1)}, bf16[96,2048]{1,0:T(8,128)(2,1)S(1)}, u32[]{:S(2)}, u32[]{:S(2)}) collective-permute-start(bf16[96,2048]{1,0:T(8,128)(2,1)S(1)} %get-tuple-element.276), channel_id=1, source_target_pairs={{0,4},{1,3},{2,6},{3,1},{4,0},{5,7},{6,2},{7,5},{8,12},{9,11},{10,... | collective-permute-start | bytes 1179656 | tf_op jit(solution)/shard_map/ppermute | solution.py:726
  208.5 5.7 %collective-permute-start.7 = (bf16[48,1152]{1,0:T(8,128)(2,1)S(1)}, bf16[48,1152]{1,0:T(8,128)(2,1)S(1)}, u32[]{:S(2)}, u32[]{:S(2)}) collective-permute-start(bf16[48,1152]{1,0:T(8,128)(2,1)S(1)} %fusion.9), channel_id=1, source_target_pairs={{0,8},{1,9},{2,10},{3,11},{4,12},{5,13},{6,14},{7,15},{8,0},{9,1},... | collective-permute-start | bytes 331784 | tf_op jit(solution)/shard_map/ppermute | solution.py:726
  212.1 5.7 %collective-permute-start.5 = (bf16[48,2048]{1,0:T(8,128)(2,1)S(1)}, bf16[48,2048]{1,0:T(8,128)(2,1)S(1)}, u32[]{:S(2)}, u32[]{:S(2)}) collective-permute-start(bf16[48,2048]{1,0:T(8,128)(2,1)S(1)} %fusion.7), channel_id=1, source_target_pairs={{0,8},{1,9},{2,10},{3,11},{4,12},{5,13},{6,14},{7,15},{8,0},{9,1},... | collective-permute-start | bytes 589832 | tf_op jit(solution)/shard_map/ppermute | solution.py:726
  217.9 14.1 %collective-permute-start.8 = (bf16[48,2048]{1,0:T(8,128)(2,1)S(1)}, bf16[48,2048]{1,0:T(8,128)(2,1)S(1)}, u32[]{:S(2)}, u32[]{:S(2)}) collective-permute-start(bf16[48,2048]{1,0:T(8,128)(2,1)S(1)} %fusion.3), channel_id=1, source_target_pairs={{0,16},{1,17},{2,18},{3,19},{4,20},{5,21},{6,22},{7,23},{8,24},{9,... | collective-permute-start | bytes 589832 | tf_op jit(solution)/shard_map/ppermute | solution.py:726
  219.5 12.6 %collective-permute-start.9 = (bf16[48,1152]{1,0:T(8,128)(2,1)S(1)}, bf16[48,1152]{1,0:T(8,128)(2,1)S(1)}, u32[]{:S(2)}, u32[]{:S(2)}) collective-permute-start(bf16[48,1152]{1,0:T(8,128)(2,1)S(1)} %fusion.5), channel_id=1, source_target_pairs={{0,16},{1,17},{2,18},{3,19},{4,20},{5,21},{6,22},{7,23},{8,24},{9,... | collective-permute-start | bytes 331784 | tf_op jit(solution)/shard_map/ppermute | solution.py:726
  232.2 7.8 %collective-permute-start.10 = (bf16[48,2048]{1,0:T(8,128)(2,1)S(1)}, bf16[48,2048]{1,0:T(8,128)(2,1)S(1)}, u32[]{:S(2)}, u32[]{:S(2)}) collective-permute-start(bf16[48,2048]{1,0:T(8,128)(2,1)S(1)} %add_convert_fusion.8), channel_id=1, source_target_pairs={{0,8},{1,9},{2,10},{3,11},{4,12},{5,13},{6,14},{7,15},{8,0},{9,1},... | collective-permute-start | bytes 589832 | tf_op jit(solution)/shard_map/ppermute | solution.py:726
  233.1 6.8 %collective-permute-start.11 = (bf16[48,1152]{1,0:T(8,128)(2,1)S(1)}, bf16[48,1152]{1,0:T(8,128)(2,1)S(1)}, u32[]{:S(2)}, u32[]{:S(2)}) collective-permute-start(bf16[48,1152]{1,0:T(8,128)(2,1)S(1)} %add_convert_fusion.11), channel_id=1, source_target_pairs={{0,8},{1,9},{2,10},{3,11},{4,12},{5,13},{6,14},{7,15},{8,0},{9,1},... | collective-permute-start | bytes 331784 | tf_op jit(solution)/shard_map/ppermute | solution.py:726
  238.2 4.9 %copy-start.17 = (f32[12,32]{1,0:T(8,128)S(1)}, f32[12,32]{1,0:T(8,128)}, u32[]{:S(2)}) copy-start(f32[12,32]{1,0:T(8,128)} %table_back.1) | copy-start | bytes 4612
  240.1 10.6 %collective-permute-start.12 = (bf16[96,2048]{1,0:T(8,128)(2,1)S(1)}, bf16[96,2048]{1,0:T(8,128)(2,1)S(1)}, u32[]{:S(2)}, u32[]{:S(2)}) collective-permute-start(bf16[96,2048]{1,0:T(8,128)(2,1)S(1)} %pad_maximum_fusion.3), channel_id=1, source_target_pairs={{0,4},{1,3},{2,6},{3,1},{4,0},{5,7},{6,2},{7,5},{8,12},{9,11},{10,... | collective-permute-start | bytes 1179656 | tf_op jit(solution)/shard_map/ppermute | solution.py:726
  243.9 16.6 %all-to-all-start.6 = ((f32[32,16,128]{2,1,0:T(8,128)}), f32[32,16,128]{2,1,0:T(8,128)S(1)}, u32[]{:S(2)}, u32[]{:S(2)}) async-start(f32[32,16,128]{2,1,0:T(8,128)} %broadcast_in_dim.14), calls=%async_computation.6 | async-start | bytes 524288 | tf_op jit(solution)/shard_map/all_to_all | solution.py:867
  248.9 9.8 %collective-permute-start.14 = (bf16[96,1152]{1,0:T(8,128)(2,1)S(1)}, bf16[96,1152]{1,0:T(8,128)(2,1)S(1)}, u32[]{:S(2)}, u32[]{:S(2)}) collective-permute-start(bf16[96,1152]{1,0:T(8,128)(2,1)S(1)} %pad_maximum_fusion.4), channel_id=1, source_target_pairs={{0,4},{1,3},{2,6},{3,1},{4,0},{5,7},{6,2},{7,5},{8,12},{9,11},{10,... | collective-permute-start | bytes 663560 | tf_op jit(solution)/shard_map/ppermute | solution.py:726
  250.8 11.6 %copy-start.3 = (bf16[192,2048]{1,0:T(8,128)(2,1)}, bf16[192,2048]{1,0:T(8,128)(2,1)S(1)}, u32[]{:S(2)}) copy-start(bf16[192,2048]{1,0:T(8,128)(2,1)S(1)} %pad_maximum_fusion.1.own_a) | copy-start | bytes 2359300
  250.8 11.6 %collective-permute-start.16 = (bf16[192,2048]{1,0:T(8,128)(2,1)S(1)}, bf16[192,2048]{1,0:T(8,128)(2,1)S(1)}, u32[]{:S(2)}, u32[]{:S(2)}) collective-permute-start(bf16[192,2048]{1,0:T(8,128)(2,1)S(1)} %pad_maximum_fusion.1.own_a), channel_id=1, source_target_pairs={{0,1},{1,0},{2,3},{3,2},{4,5},{5,4},{6,7},{7,6},{8,9},{9,8},{10,11... | collective-permute-start | bytes 2359304 | tf_op jit(solution)/shard_map/ppermute | solution.py:726
  250.9 19.3 %collective-permute-start.13 = (bf16[192,2048]{1,0:T(8,128)(2,1)S(1)}, bf16[192,2048]{1,0:T(8,128)(2,1)S(1)}, u32[]{:S(2)}, u32[]{:S(2)}) collective-permute-start(bf16[192,2048]{1,0:T(8,128)(2,1)S(1)} %pad_maximum_fusion.1.own_a), channel_id=1, source_target_pairs={{0,2},{1,5},{2,0},{3,7},{4,6},{5,1},{6,4},{7,3},{8,10},{9,13},{10,... | collective-permute-start | bytes 2359304 | tf_op jit(solution)/shard_map/ppermute | solution.py:726
  258.7 3.7 %copy-start.4 = (bf16[192,1152]{1,0:T(8,128)(2,1)}, bf16[192,1152]{1,0:T(8,128)(2,1)S(1)}, u32[]{:S(2)}) copy-start(bf16[192,1152]{1,0:T(8,128)(2,1)S(1)} %pad_maximum_fusion.2.own_b) | copy-start | bytes 1327108
  258.8 3.6 %collective-permute-start.17 = (bf16[192,1152]{1,0:T(8,128)(2,1)S(1)}, bf16[192,1152]{1,0:T(8,128)(2,1)}, u32[]{:S(2)}, u32[]{:S(2)}) collective-permute-start(bf16[192,1152]{1,0:T(8,128)(2,1)S(1)} %pad_maximum_fusion.2.own_b), channel_id=1, source_target_pairs={{0,1},{1,0},{2,3},{3,2},{4,5},{5,4},{6,7},{7,6},{8,9},{9,8},{10,11... | collective-permute-start | bytes 1327112 | tf_op jit(solution)/shard_map/ppermute | solution.py:726
  258.8 11.3 %collective-permute-start.15 = (bf16[192,1152]{1,0:T(8,128)(2,1)S(1)}, bf16[192,1152]{1,0:T(8,128)(2,1)}, u32[]{:S(2)}, u32[]{:S(2)}) collective-permute-start(bf16[192,1152]{1,0:T(8,128)(2,1)S(1)} %pad_maximum_fusion.2.own_b), channel_id=1, source_target_pairs={{0,2},{1,5},{2,0},{3,7},{4,6},{5,1},{6,4},{7,3},{8,10},{9,13},{10,... | collective-permute-start | bytes 1327112 | tf_op jit(solution)/shard_map/ppermute | solution.py:726
  262.4 0.9 copy-start.13
  270.2 3.1 %copy-start.8 = (bf16[192,2048]{1,0:T(8,128)(2,1)}, bf16[192,2048]{1,0:T(8,128)(2,1)S(1)}, u32[]{:S(2)}) copy-start(bf16[192,2048]{1,0:T(8,128)(2,1)S(1)} %collective-permute-done.13.own_a) | copy-start | bytes 2359300
  270.2 3.1 %collective-permute-start.18 = (bf16[192,2048]{1,0:T(8,128)(2,1)S(1)}, bf16[192,2048]{1,0:T(8,128)(2,1)S(1)}, u32[]{:S(2)}, u32[]{:S(2)}) collective-permute-start(bf16[192,2048]{1,0:T(8,128)(2,1)S(1)} %collective-permute-done.13.own_a), channel_id=1, source_target_pairs={{0,1},{1,0},{2,3},{3,2},{4,5},{5,4},{6,7},{7,6},{8,9},{9,8},{10,11... | collective-permute-start | bytes 2359304 | tf_op jit(solution)/shard_map/ppermute | solution.py:726
  270.3 3.0 %collective-permute-start.19 = (bf16[192,1152]{1,0:T(8,128)(2,1)}, bf16[192,1152]{1,0:T(8,128)(2,1)S(1)}, u32[]{:S(2)}, u32[]{:S(2)}) collective-permute-start(bf16[192,1152]{1,0:T(8,128)(2,1)} %collective-permute-done.15.own_b), channel_id=1, source_target_pairs={{0,1},{1,0},{2,3},{3,2},{4,5},{5,4},{6,7},{7,6},{8,9},{9,8},{10,11... | collective-permute-start | bytes 1327112 | tf_op jit(solution)/shard_map/ppermute | solution.py:726
  273.3 0.8 copy-start.15
  274.1 0.9 copy-start.9
where the time goes:
time: 283 us; the launch traced here: 281 us
  Pallas kernels  139 us (49%)
  waiting for transfers between devices  61.6 us (22%)
  starting transfers between devices  53.6 us (19%)
  local copies, waits for them, and re-layouts  14 us (5%)
  other arithmetic  12.3 us (4%)
    pallas_call x2, Pallas kernels, expert(): pl.pallas_call(functools.partial(expert_kernel, n_in=len(earlier)), grid=...  36 us
    all_to_all x7, starting transfers between devices, exchange(): return lax.all_to_all(rows, AXES, split_axis=0, concat_axis=0, tiled=True)  32.4 us
    ppermute x20, waiting for transfers between devices, swap(): return lax.ppermute(value, AXES, pairs)  31.5 us
    all_to_all x7, waiting for transfers between devices, exchange(): return lax.all_to_all(rows, AXES, split_axis=0, concat_axis=0, tiled=True)  30.1 us
    pallas_call x1, Pallas kernels, attend(): pl.pallas_call(functools.partial(attend_kernel, scaling=(width // n_heads...  26.2 us
    ppermute x20, starting transfers between devices, swap(): return lax.ppermute(value, AXES, pairs)  21.2 us
    pallas_call x1, Pallas kernels, back(): pl.pallas_call(functools.partial(back_kernel, scaling=(width // n_heads)...  20.4 us
    pallas_call x1, Pallas kernels, weights_back(): pl.pallas_call(weights_kernel, grid=(ff // block,), in_specs=[whole(n, wi...  16.8 us
  transfers between devices with their start and end apart: 27, of which 15 were waited for; matrix products, arithmetic and copies ran while one was open for 7% of the time, Pallas kernels for 46%

commit v1 on v0

--- a/solution.py
+++ b/solution.py
@@ -745,7 +745,7 @@
         return jnp.stack([me & 1] + sides)
 
 
-def unpack_kernel(where_ref, own_a, core_a, own_b, core_b, *refs):
+def unpack_kernel(where_ref, own_a, core_a, own_b, core_b, *refs, late):
     mine = pl.program_id(0) == where_ref[0]
     rows_a = jnp.where(mine, own_a[...], core_a[...]).astype(F32)
     rows_b = jnp.where(mine, own_b[...], core_b[...]).astype(F32)
@@ -754,8 +754,21 @@
     outs[3][...] = rows_a[:, :width]
     span = 128
     half = rows_b.shape[1] // 3
-    rest = width + 3 * half
-    outs[4][...] = rows_a[:, rest : rest + outs[4].shape[1]]
+    routed = rows_a[:, width + 3 * half :].T[: outs[4].shape[0], :]
+    size = routed.shape[1]
+    side = jnp.where(mine, where_ref[1], where_ref[2])
+    quarter = 2 * pl.program_id(0) + (1 - side if late else side)
+
+    @pl.when(pl.program_id(0) == 0)
+    def _():
+        outs[4][...] = refs[0][...] if late else jnp.zeros_like(outs[4])
+
+    for at in range(4):
+
+        @pl.when(quarter == at)
+        def _():
+            outs[4][:, at * size : (at + 1) * size] = routed
+
     for i in range(3):
         for p in range(half // span):
             at = (3 * p + i) * span
@@ -767,31 +780,29 @@
 
 def unpack(where, own_a, core_a, own_b, core_b, late, earlier, width, n_experts):
     rows = own_a.shape[0]
-    parts = 1
-    size = rows // parts
     earlier = tuple(earlier)
 
-    def place(c, r, where_ref):
+    def place(c, where_ref):
         side = jnp.where(c == where_ref[0], where_ref[1], where_ref[2])
-        return (2 * c + (1 - side if late else side)) * parts + r, 0
-
-    piece = lambda value: pl.BlockSpec((size, value.shape[1]), lambda c, r, where_ref: (r, 0))
+        return 2 * c + (1 - side if late else side), 0
+
+    whole = lambda *dims: pl.BlockSpec(dims, lambda c, where_ref: (0, 0))
+    inputs = (own_a, core_a, own_b, core_b) + earlier[4:]
     return pl.pallas_call(
-        unpack_kernel,
+        functools.partial(unpack_kernel, late=late),
         grid_spec=pltpu.PrefetchScalarGridSpec(
             num_scalar_prefetch=1,
-            grid=(2, parts),
-            in_specs=[piece(value) for value in (own_a, core_a, own_b, core_b)]
-            + [pl.BlockSpec(memory_space=pl.ANY)] * len(earlier),
-            out_specs=[pl.BlockSpec((size, width), place)] * 4
-            + [pl.BlockSpec((size, n_experts), place)],
+            grid=(2,),
+            in_specs=[whole(*value.shape) for value in inputs]
+            + [pl.BlockSpec(memory_space=pl.ANY)] * len(earlier[:4]),
+            out_specs=[pl.BlockSpec((rows, width), place)] * 4 + [whole(n_experts, width)],
         ),
-        out_shape=[shape((width, width), F32)] * 4 + [shape((width, n_experts), F32)],
-        input_output_aliases={5 + i: i for i in range(len(earlier))},
-        compiler_params=params(),
+        out_shape=[shape((width, width), F32)] * 4 + [shape((n_experts, width), F32)],
+        input_output_aliases={6 + i: i for i in range(len(earlier[:4]))},
+        compiler_params=pltpu.CompilerParams(vmem_limit_bytes=24 * 1024 * 1024),
         cost_estimate=cost(rows * width, 24 * rows * width),
         name="unpack",
-    )(where, own_a, core_a, own_b, core_b, *earlier)
+    )(where, *inputs, *earlier[:4])
 
 
 def tokens_kernel(grads_ref, wt_ref, tok_ref, gain_ref, dmid_ref, out_ref, gain_out, sum_s):
@@ -951,8 +962,9 @@
     )
 
     def step(kept, got, shifts):
-        kept, got = ring.cut(kept, rank, shifts), ring.cut(got, rank, shifts)
-        return [add(left, right) for left, right in zip(kept, got)]
+        sent = add(ring.cut(kept, rank, shifts)[0], ring.cut(got, rank, shifts)[0])
+        sent, kept, got = tie(sent, kept, got)
+        return sent, add(ring.cut(kept, rank, shifts)[1], ring.cut(got, rank, shifts)[1])
 
     got_a = ring.swap(sent_a, ring.core)
     sent_a, kept_a = step(kept_a, got_a, ring.plane[0])
@@ -960,42 +972,35 @@
     got_b, sent_a = tie(got_b, sent_a)
     got_a = ring.swap(sent_a, ring.plane[0])
     sent_b, kept_b = step(kept_b, got_b, ring.plane[0])
-    sent_b, grads = tie(sent_b, grads)
+    sent_b, grads, dscores = tie(sent_b, grads, dscores)
     got_b = ring.swap(sent_b, ring.plane[0])
     grad_tokens, attn_gain_rows = tokens_back(grads, weights_t, tokens, attn_gain, dmid)
-    got_a, got_b, grad_tokens, attn_gain_rows, res_rows = tie(
-        got_a, got_b, grad_tokens, attn_gain_rows, res_rows
+    grad_table = table_back(dscores, bucket_ids, n_buckets)
+    got_a, got_b, grad_tokens, attn_gain_rows, grad_table, res_rows = tie(
+        got_a, got_b, grad_tokens, attn_gain_rows, grad_table, res_rows
     )
     for shifts in ring.plane[1:] + [ring.near]:
         sent_a, kept_a = step(kept_a, got_a, shifts)
         sent_b, kept_b = step(kept_b, got_b, shifts)
         got_a, got_b = ring.swap(sent_a, shifts), ring.swap(sent_b, shifts)
     value_a, value_b = add(kept_a, got_a), add(kept_b, got_b)
-    value_a, value_b, dscores = tie(value_a, value_b, dscores)
+    value_a, value_b, grad_table, res_rows = tie(value_a, value_b, grad_table, res_rows)
     got_a, got_b = ring.swap(value_a, ring.far), ring.swap(value_b, ring.far)
-    grad_table = table_back(dscores, bucket_ids, n_buckets)
-    got_a, got_b, grad_table = tie(got_a, got_b, grad_table)
+    smalls = sum_small(
+        (attn_gain_rows[0], grad_table, moe_gain_rows[0], grad_router_bias), n_grp * n_loc
+    )
+    layer_out = leave(res_rows, col, middle)
+    got_a, got_b, layer_out = tie(got_a, got_b, layer_out)
     value_a, value_b = add(value_a, got_a), add(value_b, got_b)
-    for place, shifts in enumerate(reversed(ring.plane[1:] + [ring.near])):
-        if place == 0:
-            value_a, value_b, res_rows = tie(value_a, value_b, res_rows)
-        if place == 1:
-            value_a, value_b, grad_table = tie(value_a, value_b, grad_table)
+    for shifts in reversed(ring.plane[1:] + [ring.near]):
         got_a, got_b = ring.swap(value_a, shifts), ring.swap(value_b, shifts)
-        if place == 0:
-            layer_out = leave(res_rows, col, middle)
-            got_a, got_b, layer_out = tie(got_a, got_b, layer_out)
-        if place == 1:
-            smalls = sum_small(
-                (attn_gain_rows[0], grad_table, moe_gain_rows[0], grad_router_bias), n_grp * n_loc
-            )
         value_a = ring.join(value_a, got_a, rank, shifts)
         value_b = ring.join(value_b, got_b, rank, shifts)
+    value_a, value_b, *smalls = tie(value_a, value_b, *smalls)
     near_a, near_b = ring.swap(value_a, ring.plane[0]), ring.swap(value_b, ring.plane[0])
     core_a, core_b = ring.swap(value_a, ring.core), ring.swap(value_b, ring.core)
     outs = unpack(where, value_a, core_a, value_b, core_b, False, (), width, n_experts)
-    near_a, near_b, *rest = tie(near_a, near_b, *outs, *smalls)
-    outs, smalls = rest[:5], rest[5:]
+    near_a, near_b, *outs = tie(near_a, near_b, *outs)
     far_a, far_b = ring.swap(near_a, ring.core), ring.swap(near_b, ring.core)
     outs = unpack(where, near_a, far_a, near_b, far_b, True, outs, width, n_experts)
     grad_query, grad_key, grad_value, grad_output, grad_router = outs
@@ -1010,7 +1015,7 @@
         grad_attn_gain,
         grad_table.T,
         grad_moe_gain,
-        grad_router,
+        grad_router.T,
         grad_router_bias,
         grad_expert_in[None],
         grad_expert_out[None],

time: 283 us -> 277 us (0.979)
  waiting for transfers between devices: 61.6 us -> 68.9 us
  local copies, waits for them, and re-layouts: 14 us -> 8.59 us
  Pallas kernels: 139 us -> 136 us
  starting transfers between devices: 53.6 us -> 50.6 us
    ppermute x20, waiting for transfers between devices: 31.5 us -> 38.3 us  [swap(): return lax.ppermute(value, AXES, pairs)]
    unnamed x44 -> x33, local copies, waits for them, and re-layouts: 7.41 us -> 1.95 us
    pallas_call x2, Pallas kernels: 9.32 us -> 6.4 us  [unpack(): pl.pallas_call(functools.partial(unpack_kernel, late=late), grid_spec=plt...]
    ppermute x20, starting transfers between devices: 21.2 us -> 18.2 us  [swap(): return lax.ppermute(value, AXES, pairs)]
    convert_element_type x10 -> x14, other arithmetic: 9.97 us -> 8.41 us  [add(): return (left.astype(F32) + right.astype(F32)).astype(LOW)]
  transfers between devices with their start and end apart: 27 -> 27, of which waited for: 15 -> 16; matrix products, arithmetic and copies ran while one was open for 7% -> 6% of each run, Pallas kernels for 46% -> 47%
where the time goes in v1:
time: 277 us; the launch traced here: 276 us
  Pallas kernels  136 us (49%)
  waiting for transfers between devices  68.9 us (25%)
  starting transfers between devices  50.6 us (18%)
  other arithmetic  10.3 us (4%)
  local copies, waits for them, and re-layouts  8.59 us (3%)
    ppermute x20, waiting for transfers between devices, swap(): return lax.ppermute(value, AXES, pairs)  38.3 us
    pallas_call x2, Pallas kernels, expert(): pl.pallas_call(functools.partial(expert_kernel, n_in=len(earlier)), grid=...  36 us
    all_to_all x7, starting transfers between devices, exchange(): return lax.all_to_all(rows, AXES, split_axis=0, concat_axis=0, tiled=True)  32.4 us
    all_to_all x7, waiting for transfers between devices, exchange(): return lax.all_to_all(rows, AXES, split_axis=0, concat_axis=0, tiled=True)  30.6 us
    pallas_call x1, Pallas kernels, attend(): pl.pallas_call(functools.partial(attend_kernel, scaling=(width // n_heads...  26.2 us
    pallas_call x1, Pallas kernels, back(): pl.pallas_call(functools.partial(back_kernel, scaling=(width // n_heads)...  20.5 us
    ppermute x20, starting transfers between devices, swap(): return lax.ppermute(value, AXES, pairs)  18.2 us
    pallas_call x1, Pallas kernels, weights_back(): pl.pallas_call(weights_kernel, grid=(ff // block,), in_specs=[whole(n, wi...  16.8 us
  transfers between devices with their start and end apart: 27, of which 16 were waited for; matrix products, arithmetic and copies ran while one was open for 6% of the time, Pallas kernels for 47%

profile of v1, /device:TPU:0, one launch (start us, length us, event | category | flops | bytes accessed | tf_op | source)
XLA Modules:
  0.0 275.7 jit_solution(11096722437749816483)
XLA Ops:
  0.6 3.8 %dispatch.1 = (bf16[1024,768]{1,0:T(8,128)(2,1)}, s32[8,512]{1,0:T(8,128)}, s32[512,128]{1,0:T(8,128)}) custom-call(s32[1,512]{1,0:T(1,128)} %bitcast.123, bf16[512,768]{1,0:T(8,128)(2,1)} %dy_hbm.1), custom_call_target="tpu_custom_call" | custom-call | flops 805306368 | bytes 3145728 | tf_op jit(solution)/shard_map/dispatch/pallas_call | solution.py:79
  4.5 7.3 %all-to-all-start = ((bf16[32,32,768]{2,1,0:T(8,128)(2,1)}), bf16[32,32,768]{2,1,0:T(8,128)(2,1)S(1)}, u32[]{:S(2)}, u32[]{:S(2)}) async-start(bf16[32,32,768]{2,1,0:T(8,128)(2,1)} %bitcast.97), calls=%async_computation | async-start | bytes 3145728 | tf_op jit(solution)/shard_map/all_to_all | solution.py:878
  13.6 26.2 %attend.1 = (bf16[512,768]{1,0:T(8,128)(2,1)}, bf16[512,768]{1,0:T(8,128)(2,1)}, bf16[512,768]{1,0:T(8,128)(2,1)}, bf16[12,512,512]{2,1,0:T(8,128)(2,1)}, bf16[7...) custom-call(bf16[512,768]{1,0:T(8,128)(2,1)} %tok_ref.3, ...), custom_call_target="tpu_custom_call" | custom-call | flops 4831838208 | bytes 15728640 | tf_op jit(solution)/shard_map/attend/pallas_call | solution.py:179
  39.8 9.5 %all-to-all-done = bf16[32,32,768]{2,1,0:T(8,128)(2,1)S(1)} async-done(((bf16[32,32,768]{2,1,0:T(8,128)(2,1)}), bf16[32,32,768]{2,1,0:T(8,128)(2,1)S(1)}, u32[]{:S(2)}, u32[]{:S(2)}) %all-to-all-start) | async-done | bytes 1572896 | tf_op jit(solution)/shard_map/all_to_all | solution.py:878
  49.3 3.7 %all-to-all-start.1 = ((bf16[32,16,768]{2,1,0:T(8,128)(2,1)}), bf16[32,16,768]{2,1,0:T(8,128)(2,1)S(1)}, u32[]{:S(2)}, u32[]{:S(2)}) async-start(bf16[32,16,768]{2,1,0:T(8,128)(2,1)} %bitcast.109), calls=%async_computation.1 | async-start | bytes 1572864 | tf_op jit(solution)/shard_map/all_to_all | solution.py:878
  53.0 5.2 %arrive.1 = (bf16[512,768]{1,0:T(8,128)(2,1)}, bf16[512,768]{1,0:T(8,128)(2,1)}, f32[512,128]{1,0:T(8,128)}, f32[512,128]{1,0:T(8,128)}) custom-call(bf16[1024,768]{1,0:T(8,128)(2,1)} %bitcast.96), custom_call_target="tpu_custom_call" | custom-call | flops 1610612736 | bytes 3145728 | tf_op jit(solution)/shard_map/arrive/pallas_call | solution.py:263
  58.2 15.4 %all-to-all-done.1 = bf16[32,16,768]{2,1,0:T(8,128)(2,1)S(1)} async-done(((bf16[32,16,768]{2,1,0:T(8,128)(2,1)}), bf16[32,16,768]{2,1,0:T(8,128)(2,1)S(1)}, u32[]{:S(2)}, u32[]{:S(2)}) %all-to-all-start.1) | async-done | bytes 786464 | tf_op jit(solution)/shard_map/all_to_all | solution.py:878
  73.6 3.8 %all-to-all-start.2 = ((bf16[32,16,768]{2,1,0:T(8,128)(2,1)}), bf16[32,16,768]{2,1,0:T(8,128)(2,1)S(1)}, u32[]{:S(2)}, u32[]{:S(2)}) async-start(bf16[32,16,768]{2,1,0:T(8,128)(2,1)} %bitcast.8), calls=%async_computation.2 | async-start | bytes 1572864 | tf_op jit(solution)/shard_map/all_to_all | solution.py:878
  78.4 18.0 %expert.2 = (bf16[512,768]{1,0:T(8,128)(2,1)}, bf16[512,768]{1,0:T(8,128)(2,1)}, bf16[1024,3072]{1,0:T(8,128)(2,1)}, bf16[1024,3072]{1,0:T(8,128)(2,1)}, bf16[1024,768]{1,0:T(8,128)(2,1)}, /*index=5*/f32[1024,32]{1,0:T(8,128)}) custom-call(s32[1]{0:T(128)} %bitcast.me_ref, bf16[512,768]{1,0:T(8,128)(2,1)} %bitcast.104, ...), custom_call_target="tpu_custom_call" | custom-call | flops 9663676416 | bytes 37748736 | tf_op jit(solution)/shard_map/expert/pallas_call | solution.py:338
  96.3 1.5 all-to-all-done.2
  97.9 4.2 %all-to-all-start.3 = ((bf16[32,16,768]{2,1,0:T(8,128)(2,1)}), bf16[32,16,768]{2,1,0:T(8,128)(2,1)S(1)}, u32[]{:S(2)}, u32[]{:S(2)}) async-start(bf16[32,16,768]{2,1,0:T(8,128)(2,1)} %bitcast.110), calls=%async_computation.3 | async-start | bytes 1572864 | tf_op jit(solution)/shard_map/all_to_all | solution.py:878
  102.0 18.0 %expert.3 = (bf16[512,768]{1,0:T(8,128)(2,1)}, bf16[512,768]{1,0:T(8,128)(2,1)}, bf16[1024,3072]{1,0:T(8,128)(2,1)}, bf16[1024,3072]{1,0:T(8,128)(2,1)}, bf16[1024,768]{1,0:T(8,128)(2,1)}, /*index=5*/f32[1024,32]{1,0:T(8,128)}) custom-call(s32[1]{0:T(128)} %bitcast.me_ref, ...), custom_call_target="tpu_custom_call", output_to_operand_aliasing={{2}: (8, {}), {3}: (9, {}), {4}: (10, {}), {5}: (11, {})} | custom-call | flops 9663676416 | bytes 37748736 | tf_op jit(solution)/shard_map/expert/pallas_call | solution.py:338
  120.1 2.6 all-to-all-done.3
  122.7 3.6 %all-to-all-start.4 = ((bf16[32,16,768]{2,1,0:T(8,128)(2,1)}), bf16[32,16,768]{2,1,0:T(8,128)(2,1)S(1)}, u32[]{:S(2)}, u32[]{:S(2)}) async-start(bf16[32,16,768]{2,1,0:T(8,128)(2,1)} %bitcast.108), calls=%async_computation.4 | async-start | bytes 1572864 | tf_op jit(solution)/shard_map/all_to_all | solution.py:878
  126.4 1.4 pad_maximum_fusion
  127.7 16.8 %weights_back.1 = (f32[768,3072]{1,0:T(8,128)}, f32[3072,768]{1,0:T(8,128)}, f32[768,128]{1,0:T(8,128)}, f32[8,32]{1,0:T(8,128)}) custom-call(bf16[512,768]{1,0:T(8,128)(2,1)} %bitcast.105, bf16[512,768]{1,0:T(8,128)(2,1)} %bitcast.107, bf16[1024,3072]{1,0:T(8,128)(2,1)} %get-tuple-element.180.hid_ref, bf16[1024,3072]{1,0:T(8,128)(2,1)} %get-tuple-element.181.dpre_ref, ...), custom_call_target="tpu_custom_call" | custom-call | flops 9663676416 | bytes 18874368 | tf_op jit(solution)/shard_map/weights_back/pallas_call | solution.py:409
  145.3 1.6 all-to-all-done.4
  147.9 4.4 %all-to-all-start.5 = ((bf16[32,32,768]{2,1,0:T(8,128)(2,1)}), bf16[32,32,768]{2,1,0:T(8,128)(2,1)S(1)}, u32[]{:S(2)}, u32[]{:S(2)}) async-start(bf16[32,32,768]{2,1,0:T(8,128)(2,1)} %bitcast.30), calls=%async_computation.5 | async-start | bytes 3145728 | tf_op jit(solution)/shard_map/all_to_all | solution.py:878
  152.3 20.5 %back.1 = (f32[512,768]{1,0:T(8,128)}, bf16[384,2048]{1,0:T(8,128)(2,1)}, bf16[384,2048]{1,0:T(8,128)(2,1)}, f32[8,768]{1,0:T(8,128)}, bf16[512,2304]{1,0:T(8,12...) custom-call(s32[1]{0:T(128)S(6)} %and.16.core_ref, ...), custom_call_target="tpu_custom_call" | custom-call | flops 1000 | bytes 1000 | tf_op jit(solution)/shard_map/back/pallas_call | solution.py:619
  174.2 3.5 %collective-permute-done = bf16[384,2048]{1,0:T(8,128)(2,1)S(1)} collective-permute-done((bf16[384,2048]{1,0:T(8,128)(2,1)}, bf16[384,2048]{1,0:T(8,128)(2,1)S(1)}, u32[]{:S(2)}, u32[]{:S(2)}) %collective-permute-start) | collective-permute-done | bytes 1572896 | tf_op jit(solution)/shard_map/ppermute | solution.py:726
  177.8 1.9 fusion
  179.7 1.3 fusion.1
  181.0 1.1 collective-permute-start.3
  183.1 1.1 add_convert_fusion.2
  184.3 1.4 add_convert_fusion
  185.7 7.2 %tokens_back.1 = (bf16[512,768]{1,0:T(8,128)(2,1)}, f32[8,768]{1,0:T(8,128)}) custom-call(bf16[512,2304]{1,0:T(8,128)(2,1)} %get-tuple-element.211.grads_ref, bf16[2304,768]{1,0:T(8,128)(2,1)} %get-tuple-element.212.wt_ref, bf16[512,768]{1,0:T(8,128)(2,1)} %tok_ref.3, f32[1,768]{1,0:T(1,128)} %reshape.225.gain_ref, f32[512,768]{1,0:T(8,128)} %get-tuple-element.213.dmid_ref), custom_call_target="tpu_custom_call" | custom-call | flops 1811939328 | bytes 9043968 | tf_op jit(solution)/shard_map/tokens_back/pallas_call | solution.py:840
  192.9 10.0 %table_back.1 = f32[12,32]{1,0:T(8,128)} custom-call(bf16[12,512,512]{2,1,0:T(8,128)(2,1)} %get-tuple-element.216.ds_ref, s32[512,512]{1,0:T(8,128)} %bucket_ref.3), custom_call_target="tpu_custom_call" | custom-call | flops 3221225472 | bytes 6291456 | tf_op jit(solution)/shard_map/table_back/pallas_call | solution.py:688
  203.0 1.2 collective-permute-start.6
  206.4 1.1 add_convert_fusion.4
  207.5 1.5 collective-permute-done.6
  210.1 3.1 %collective-permute-done.4 = bf16[96,2048]{1,0:T(8,128)(2,1)S(1)} collective-permute-done((bf16[96,2048]{1,0:T(8,128)(2,1)S(1)}, bf16[96,2048]{1,0:T(8,128)(2,1)S(1)}, u32[]{:S(2)}, u32[]{:S(2)}) %collective-permute-start.4) | collective-permute-done | bytes 393248 | tf_op jit(solution)/shard_map/ppermute | solution.py:726
  213.3 1.3 collective-permute-start.5
  214.7 4.4 %collective-permute-done.5 = bf16[48,2048]{1,0:T(8,128)(2,1)S(1)} collective-permute-done((bf16[48,2048]{1,0:T(8,128)(2,1)S(1)}, bf16[48,2048]{1,0:T(8,128)(2,1)S(1)}, u32[]{:S(2)}, u32[]{:S(2)}) %collective-permute-start.5) | collective-permute-done | bytes 196640 | tf_op jit(solution)/shard_map/ppermute | solution.py:726
  219.1 2.3 collective-permute-start.8
  223.7 5.4 %all-to-all-start.6 = ((f32[32,16,128]{2,1,0:T(8,128)}), f32[32,16,128]{2,1,0:T(8,128)S(1)}, u32[]{:S(2)}, u32[]{:S(2)}) async-start(f32[32,16,128]{2,1,0:T(8,128)} %broadcast_in_dim.14), calls=%async_computation.6 | async-start | bytes 524288 | tf_op jit(solution)/shard_map/all_to_all | solution.py:878
  229.0 4.0 %leave.1 = bf16[512,768]{1,0:T(8,128)(2,1)} custom-call(bf16[1024,768]{1,0:T(8,128)(2,1)} %bitcast.85, s32[512,128]{1,0:T(8,128)} %get-tuple-element.189.col_hbm.col_ref, f32[512,768]{1,0:T(8,128)} %get-tuple-element.190.mid_hbm.mid_ref), custom_call_target="tpu_custom_call" | custom-call | flops 805306368 | bytes 3932160 | tf_op jit(solution)/shard_map/leave/pallas_call | solution.py:868
  233.0 2.0 collective-permute-done.9
  235.1 1.6 collective-permute-start.12
  237.3 4.0 %collective-permute-done.12 = bf16[48,1152]{1,0:T(8,128)(2,1)S(1)} collective-permute-done((bf16[48,1152]{1,0:T(8,128)(2,1)S(1)}, bf16[48,1152]{1,0:T(8,128)(2,1)S(1)}, u32[]{:S(2)}, u32[]{:S(2)}) %collective-permute-start.12) | collective-permute-done | bytes 110624 | tf_op jit(solution)/shard_map/ppermute | solution.py:726
  242.3 2.2 collective-permute-done.10
  244.6 1.3 collective-permute-start.11
  247.9 4.5 %collective-permute-done.11 = bf16[96,2048]{1,0:T(8,128)(2,1)S(1)} collective-permute-done((bf16[96,2048]{1,0:T(8,128)(2,1)S(1)}, bf16[96,2048]{1,0:T(8,128)(2,1)S(1)}, u32[]{:S(2)}, u32[]{:S(2)}) %collective-permute-start.11) | collective-permute-done | bytes 393248 | tf_op jit(solution)/shard_map/ppermute | solution.py:726
  252.7 1.4 collective-permute-start.14
  254.2 1.6 collective-permute-start.15
  255.9 3.1 %unpack.2 = (f32[768,768]{1,0:T(8,128)}, f32[768,768]{1,0:T(8,128)}, f32[768,768]{1,0:T(8,128)}, f32[768,768]{1,0:T(8,128)}, f32[32,768]{1,0:T(8,128)S(1)}) custom-call(s32[3]{0:T(128)S(1)} %pad_add_fusion.where_ref, bf16[192,2048]{1,0:T(8,128)(2,1)S(1)} %pad_maximum_fusion.1.own_a, bf16[192,2048]{1,0:T(8,128)(2,1)S(1)} %collective-permute-done.16.core_a, ...), custom_call_target="tpu_custom_call" | custom-call | flops 147456 | bytes 3538944 | tf_op jit(solution)/shard_map/unpack/pallas_call | solution.py:791
  259.1 10.5 %collective-permute-done.15.own_b = bf16[192,1152]{1,0:T(8,128)(2,1)S(1)} collective-permute-done((bf16[192,1152]{1,0:T(8,128)(2,1)S(1)}, bf16[192,1152]{1,0:T(8,128)(2,1)S(1)}, u32[]{:S(2)}, u32[]{:S(2)}) %collective-permute-start.15) | collective-permute-done | bytes 442400 | tf_op jit(solution)/shard_map/ppermute | solution.py:726
  270.0 2.4 collective-permute-done.19.core_b
  272.4 3.3 %unpack.3 = (f32[768,768]{1,0:T(8,128)}, f32[768,768]{1,0:T(8,128)}, f32[768,768]{1,0:T(8,128)}, f32[768,768]{1,0:T(8,128)}, f32[32,768]{1,0:T(8,128)}) custom-call(s32[3]{0:T(128)S(1)} %pad_add_fusion.where_ref, bf16[192,2048]{1,0:T(8,128)(2,1)S(1)} %collective-permute-done.14.own_a, ...), custom_call_target="tpu_custom_call", output_to_operand_aliasing={{0}: (6, {}), {1}: (7, {}), {2}: (8, {}), {3}: (9, {})} | custom-call | flops 147456 | bytes 3538944 | tf_op jit(solution)/shard_map/unpack/pallas_call | solution.py:791
  (90 shorter events, 17.3 us)
Async XLA Ops:
  4.5 7.3 %copy-start.14 = (f32[768]{0:T(1024)S(1)}, f32[768]{0:T(1024)}, u32[]{:S(2)}) copy-start(f32[768]{0:T(1024)} %param.21) | copy-start | bytes 9220
  4.5 7.9 %copy-start.15 = (f32[768]{0:T(1024)S(1)}, f32[768]{0:T(1024)}, u32[]{:S(2)}) copy-start(f32[768]{0:T(1024)} %param.23) | copy-start | bytes 9220
  4.5 8.5 %copy-start.13 = (f32[32,12]{0,1:T(8,128)S(1)}, f32[32,12]{0,1:T(8,128)}, u32[]{:S(2)}) copy-start(f32[32,12]{0,1:T(8,128)} %param.22) | copy-start | bytes 4612
  4.5 44.8 %all-to-all-start = ((bf16[32,32,768]{2,1,0:T(8,128)(2,1)}), bf16[32,32,768]{2,1,0:T(8,128)(2,1)S(1)}, u32[]{:S(2)}, u32[]{:S(2)}) async-start(bf16[32,32,768]{2,1,0:T(8,128)(2,1)} %bitcast.97), calls=%async_computation | async-start | bytes 3145728 | tf_op jit(solution)/shard_map/all_to_all | solution.py:878
  49.3 3.7 %copy-start.5 = (bf16[32,32,768]{2,1,0:T(8,128)(2,1)}, bf16[32,32,768]{2,1,0:T(8,128)(2,1)S(1)}, u32[]{:S(2)}) copy-start(bf16[32,32,768]{2,1,0:T(8,128)(2,1)S(1)} %all-to-all-done) | copy-start | bytes 4718596
  49.3 24.3 %all-to-all-start.1 = ((bf16[32,16,768]{2,1,0:T(8,128)(2,1)}), bf16[32,16,768]{2,1,0:T(8,128)(2,1)S(1)}, u32[]{:S(2)}, u32[]{:S(2)}) async-start(bf16[32,16,768]{2,1,0:T(8,128)(2,1)} %bitcast.109), calls=%async_computation.1 | async-start | bytes 1572864 | tf_op jit(solution)/shard_map/all_to_all | solution.py:878
  58.2 19.2 %copy-start.11 = (f32[768,32]{0,1:T(8,128)S(1)}, f32[768,32]{0,1:T(8,128)}, u32[]{:S(2)}) copy-start(f32[768,32]{0,1:T(8,128)} %param.24) | copy-start | bytes 294916
  73.6 4.8 %copy-start.7 = (bf16[32,16,768]{2,1,0:T(8,128)(2,1)}, bf16[32,16,768]{2,1,0:T(8,128)(2,1)S(1)}, u32[]{:S(2)}) copy-start(bf16[32,16,768]{2,1,0:T(8,128)(2,1)S(1)} %all-to-all-done.1) | copy-start | bytes 2359300
  73.6 24.2 %all-to-all-start.2 = ((bf16[32,16,768]{2,1,0:T(8,128)(2,1)}), bf16[32,16,768]{2,1,0:T(8,128)(2,1)S(1)}, u32[]{:S(2)}, u32[]{:S(2)}) async-start(bf16[32,16,768]{2,1,0:T(8,128)(2,1)} %bitcast.8), calls=%async_computation.2 | async-start | bytes 1572864 | tf_op jit(solution)/shard_map/all_to_all | solution.py:878
  97.9 4.2 %copy-start.8 = (bf16[32,16,768]{2,1,0:T(8,128)(2,1)}, bf16[32,16,768]{2,1,0:T(8,128)(2,1)S(1)}, u32[]{:S(2)}) copy-start(bf16[32,16,768]{2,1,0:T(8,128)(2,1)S(1)} %all-to-all-done.2) | copy-start | bytes 2359300
  97.9 24.8 %all-to-all-start.3 = ((bf16[32,16,768]{2,1,0:T(8,128)(2,1)}), bf16[32,16,768]{2,1,0:T(8,128)(2,1)S(1)}, u32[]{:S(2)}, u32[]{:S(2)}) async-start(bf16[32,16,768]{2,1,0:T(8,128)(2,1)} %bitcast.110), calls=%async_computation.3 | async-start | bytes 1572864 | tf_op jit(solution)/shard_map/all_to_all | solution.py:878
  120.1 6.3 %copy-start.9 = (bf16[512,768]{1,0:T(8,128)(2,1)S(1)}, bf16[512,768]{1,0:T(8,128)(2,1)}, u32[]{:S(2)}) copy-start(bf16[512,768]{1,0:T(8,128)(2,1)} %get-tuple-element.178) | copy-start | bytes 2359300
  120.1 6.3 %copy-start.10 = (bf16[512,768]{1,0:T(8,128)(2,1)S(1)}, bf16[512,768]{1,0:T(8,128)(2,1)}, u32[]{:S(2)}) copy-start(bf16[512,768]{1,0:T(8,128)(2,1)} %get-tuple-element.179) | copy-start | bytes 2359300
  122.7 5.1 %copy-start.1 = (bf16[32,16,768]{2,1,0:T(8,128)(2,1)}, bf16[32,16,768]{2,1,0:T(8,128)(2,1)S(1)}, u32[]{:S(2)}) copy-start(bf16[32,16,768]{2,1,0:T(8,128)(2,1)S(1)} %all-to-all-done.3) | copy-start | bytes 2359300
  122.7 24.2 %all-to-all-start.4 = ((bf16[32,16,768]{2,1,0:T(8,128)(2,1)}), bf16[32,16,768]{2,1,0:T(8,128)(2,1)S(1)}, u32[]{:S(2)}, u32[]{:S(2)}) async-start(bf16[32,16,768]{2,1,0:T(8,128)(2,1)} %bitcast.108), calls=%async_computation.4 | async-start | bytes 1572864 | tf_op jit(solution)/shard_map/all_to_all | solution.py:878
  146.9 1.0 copy-start.2
  147.9 55.1 %all-to-all-start.5 = ((bf16[32,32,768]{2,1,0:T(8,128)(2,1)}), bf16[32,32,768]{2,1,0:T(8,128)(2,1)S(1)}, u32[]{:S(2)}, u32[]{:S(2)}) async-start(bf16[32,32,768]{2,1,0:T(8,128)(2,1)} %bitcast.30), calls=%async_computation.5 | async-start | bytes 3145728 | tf_op jit(solution)/shard_map/all_to_all | solution.py:878
  172.8 5.0 %collective-permute-start = (bf16[384,2048]{1,0:T(8,128)(2,1)}, bf16[384,2048]{1,0:T(8,128)(2,1)S(1)}, u32[]{:S(2)}, u32[]{:S(2)}) collective-permute-start(bf16[384,2048]{1,0:T(8,128)(2,1)} %get-tuple-element.199), channel_id=1, source_target_pairs={{0,1},{1,0},{2,3},{3,2},{4,5},{5,4},{6,7},{7,6},{8,9},{9,8},{10,11... | collective-permute-start | bytes 4718600 | tf_op jit(solution)/shard_map/ppermute | solution.py:726
  172.9 6.8 %collective-permute-start.1 = (bf16[384,1152]{1,0:T(8,128)(2,1)}, bf16[384,1152]{1,0:T(8,128)(2,1)}, u32[]{:S(2)}, u32[]{:S(2)}) collective-permute-start(bf16[384,1152]{1,0:T(8,128)(2,1)} %get-tuple-element.202), channel_id=1, source_target_pairs={{0,1},{1,0},{2,3},{3,2},{4,5},{5,4},{6,7},{7,6},{8,9},{9,8},{10,11... | collective-permute-start | bytes 2654216 | tf_op jit(solution)/shard_map/ppermute | solution.py:726
  173.4 6.3 %copy-start.6 = (bf16[384,1152]{1,0:T(8,128)(2,1)S(1)}, bf16[384,1152]{1,0:T(8,128)(2,1)}, u32[]{:S(2)}) copy-start(bf16[384,1152]{1,0:T(8,128)(2,1)} %get-tuple-element.225) | copy-start | bytes 2654212
  177.8 3.3 %copy-start.4 = (bf16[384,2048]{1,0:T(8,128)(2,1)}, bf16[384,2048]{1,0:T(8,128)(2,1)S(1)}, u32[]{:S(2)}) copy-start(bf16[384,2048]{1,0:T(8,128)(2,1)S(1)} %collective-permute-done) | copy-start | bytes 4718596
  179.7 4.6 %copy-start.3 = (bf16[384,2048]{1,0:T(8,128)(2,1)S(1)}, bf16[384,2048]{1,0:T(8,128)(2,1)}, u32[]{:S(2)}) copy-start(bf16[384,2048]{1,0:T(8,128)(2,1)} %get-tuple-element.200) | copy-start | bytes 4718596
  181.0 21.9 %collective-permute-start.3 = (bf16[192,1152]{1,0:T(8,128)(2,1)S(1)}, bf16[192,1152]{1,0:T(8,128)(2,1)S(1)}, u32[]{:S(2)}, u32[]{:S(2)}) collective-permute-start(bf16[192,1152]{1,0:T(8,128)(2,1)S(1)} %fusion.1), channel_id=1, source_target_pairs={{0,2},{1,5},{2,0},{3,7},{4,6},{5,1},{6,4},{7,3},{8,10},{9,13},{10,... | collective-permute-start | bytes 1327112 | tf_op jit(solution)/shard_map/ppermute | solution.py:726
  182.2 20.8 %collective-permute-start.2 = (bf16[192,2048]{1,0:T(8,128)(2,1)S(1)}, bf16[192,2048]{1,0:T(8,128)(2,1)}, u32[]{:S(2)}, u32[]{:S(2)}) collective-permute-start(bf16[192,2048]{1,0:T(8,128)(2,1)S(1)} %fusion), channel_id=1, source_target_pairs={{0,2},{1,5},{2,0},{3,7},{4,6},{5,1},{6,4},{7,3},{8,10},{9,13},{10,... | collective-permute-start | bytes 2359304 | tf_op jit(solution)/shard_map/ppermute | solution.py:726
  202.9 4.6 %copy-start = (bf16[32,32,768]{2,1,0:T(8,128)(2,1)}, bf16[32,32,768]{2,1,0:T(8,128)(2,1)S(1)}, u32[]{:S(2)}) copy-start(bf16[32,32,768]{2,1,0:T(8,128)(2,1)S(1)} %all-to-all-done.5) | copy-start | bytes 4718596
  203.0 6.0 %collective-permute-start.6 = (bf16[96,1152]{1,0:T(8,128)(2,1)S(1)}, bf16[96,1152]{1,0:T(8,128)(2,1)S(1)}, u32[]{:S(2)}, u32[]{:S(2)}) collective-permute-start(bf16[96,1152]{1,0:T(8,128)(2,1)S(1)} %fusion.4), channel_id=1, source_target_pairs={{0,4},{1,3},{2,6},{3,1},{4,0},{5,7},{6,2},{7,5},{8,12},{9,11},{10,... | collective-permute-start | bytes 663560 | tf_op jit(solution)/shard_map/ppermute | solution.py:726
  205.3 7.9 %collective-permute-start.4 = (bf16[96,2048]{1,0:T(8,128)(2,1)S(1)}, bf16[96,2048]{1,0:T(8,128)(2,1)S(1)}, u32[]{:S(2)}, u32[]{:S(2)}) collective-permute-start(bf16[96,2048]{1,0:T(8,128)(2,1)S(1)} %fusion.2), channel_id=1, source_target_pairs={{0,4},{1,3},{2,6},{3,1},{4,0},{5,7},{6,2},{7,5},{8,12},{9,11},{10,... | collective-permute-start | bytes 1179656 | tf_op jit(solution)/shard_map/ppermute | solution.py:726
  206.3 15.8 %copy-start.12 = (f32[12,32]{1,0:T(8,128)S(1)}, f32[12,32]{1,0:T(8,128)}, u32[]{:S(2)}) copy-start(f32[12,32]{1,0:T(8,128)} %table_back.1) | copy-start | bytes 4612
  209.0 5.6 %collective-permute-start.7 = (bf16[48,1152]{1,0:T(8,128)(2,1)S(1)}, bf16[48,1152]{1,0:T(8,128)(2,1)S(1)}, u32[]{:S(2)}, u32[]{:S(2)}) collective-permute-start(bf16[48,1152]{1,0:T(8,128)(2,1)S(1)} %fusion.8), channel_id=1, source_target_pairs={{0,8},{1,9},{2,10},{3,11},{4,12},{5,13},{6,14},{7,15},{8,0},{9,1},... | collective-permute-start | bytes 331784 | tf_op jit(solution)/shard_map/ppermute | solution.py:726
  213.3 5.7 %collective-permute-start.5 = (bf16[48,2048]{1,0:T(8,128)(2,1)S(1)}, bf16[48,2048]{1,0:T(8,128)(2,1)S(1)}, u32[]{:S(2)}, u32[]{:S(2)}) collective-permute-start(bf16[48,2048]{1,0:T(8,128)(2,1)S(1)} %fusion.6), channel_id=1, source_target_pairs={{0,8},{1,9},{2,10},{3,11},{4,12},{5,13},{6,14},{7,15},{8,0},{9,1},... | collective-permute-start | bytes 589832 | tf_op jit(solution)/shard_map/ppermute | solution.py:726
  219.1 15.9 %collective-permute-start.8 = (bf16[48,2048]{1,0:T(8,128)(2,1)S(1)}, bf16[48,2048]{1,0:T(8,128)(2,1)S(1)}, u32[]{:S(2)}, u32[]{:S(2)}) collective-permute-start(bf16[48,2048]{1,0:T(8,128)(2,1)S(1)} %fusion.3), channel_id=1, source_target_pairs={{0,16},{1,17},{2,18},{3,19},{4,20},{5,21},{6,22},{7,23},{8,24},{9,... | collective-permute-start | bytes 589832 | tf_op jit(solution)/shard_map/ppermute | solution.py:726
  222.2 12.8 %collective-permute-start.9 = (bf16[48,1152]{1,0:T(8,128)(2,1)S(1)}, bf16[48,1152]{1,0:T(8,128)(2,1)S(1)}, u32[]{:S(2)}, u32[]{:S(2)}) collective-permute-start(bf16[48,1152]{1,0:T(8,128)(2,1)S(1)} %fusion.5), channel_id=1, source_target_pairs={{0,16},{1,17},{2,18},{3,19},{4,20},{5,21},{6,22},{7,23},{8,24},{9,... | collective-permute-start | bytes 331784 | tf_op jit(solution)/shard_map/ppermute | solution.py:726
  223.7 22.3 %all-to-all-start.6 = ((f32[32,16,128]{2,1,0:T(8,128)}), f32[32,16,128]{2,1,0:T(8,128)S(1)}, u32[]{:S(2)}, u32[]{:S(2)}) async-start(f32[32,16,128]{2,1,0:T(8,128)} %broadcast_in_dim.14), calls=%async_computation.6 | async-start | bytes 524288 | tf_op jit(solution)/shard_map/all_to_all | solution.py:878
  235.1 6.2 %collective-permute-start.12 = (bf16[48,1152]{1,0:T(8,128)(2,1)S(1)}, bf16[48,1152]{1,0:T(8,128)(2,1)S(1)}, u32[]{:S(2)}, u32[]{:S(2)}) collective-permute-start(bf16[48,1152]{1,0:T(8,128)(2,1)S(1)} %add_convert_fusion.11), channel_id=1, source_target_pairs={{0,8},{1,9},{2,10},{3,11},{4,12},{5,13},{6,14},{7,15},{8,0},{9,1},... | collective-permute-start | bytes 331784 | tf_op jit(solution)/shard_map/ppermute | solution.py:726
  236.7 7.8 %collective-permute-start.10 = (bf16[48,2048]{1,0:T(8,128)(2,1)S(1)}, bf16[48,2048]{1,0:T(8,128)(2,1)S(1)}, u32[]{:S(2)}, u32[]{:S(2)}) collective-permute-start(bf16[48,2048]{1,0:T(8,128)(2,1)S(1)} %add_convert_fusion.8), channel_id=1, source_target_pairs={{0,8},{1,9},{2,10},{3,11},{4,12},{5,13},{6,14},{7,15},{8,0},{9,1},... | collective-permute-start | bytes 589832 | tf_op jit(solution)/shard_map/ppermute | solution.py:726
  241.4 6.4 %collective-permute-start.13 = (bf16[96,1152]{1,0:T(8,128)(2,1)S(1)}, bf16[96,1152]{1,0:T(8,128)(2,1)S(1)}, u32[]{:S(2)}, u32[]{:S(2)}) collective-permute-start(bf16[96,1152]{1,0:T(8,128)(2,1)S(1)} %pad_maximum_fusion.4), channel_id=1, source_target_pairs={{0,4},{1,3},{2,6},{3,1},{4,0},{5,7},{6,2},{7,5},{8,12},{9,11},{10,... | collective-permute-start | bytes 663560 | tf_op jit(solution)/shard_map/ppermute | solution.py:726
  244.6 7.8 %collective-permute-start.11 = (bf16[96,2048]{1,0:T(8,128)(2,1)S(1)}, bf16[96,2048]{1,0:T(8,128)(2,1)S(1)}, u32[]{:S(2)}, u32[]{:S(2)}) collective-permute-start(bf16[96,2048]{1,0:T(8,128)(2,1)S(1)} %pad_maximum_fusion.3), channel_id=1, source_target_pairs={{0,4},{1,3},{2,6},{3,1},{4,0},{5,7},{6,2},{7,5},{8,12},{9,11},{10,... | collective-permute-start | bytes 1179656 | tf_op jit(solution)/shard_map/ppermute | solution.py:726
  252.6 3.3 %collective-permute-start.16 = (bf16[192,2048]{1,0:T(8,128)(2,1)S(1)}, bf16[192,2048]{1,0:T(8,128)(2,1)S(1)}, u32[]{:S(2)}, u32[]{:S(2)}) collective-permute-start(bf16[192,2048]{1,0:T(8,128)(2,1)S(1)} %pad_maximum_fusion.1.own_a), channel_id=1, source_target_pairs={{0,1},{1,0},{2,3},{3,2},{4,5},{5,4},{6,7},{7,6},{8,9},{9,8},{10,11... | collective-permute-start | bytes 2359304 | tf_op jit(solution)/shard_map/ppermute | solution.py:726
  252.7 16.8 %collective-permute-start.14 = (bf16[192,2048]{1,0:T(8,128)(2,1)S(1)}, bf16[192,2048]{1,0:T(8,128)(2,1)S(1)}, u32[]{:S(2)}, u32[]{:S(2)}) collective-permute-start(bf16[192,2048]{1,0:T(8,128)(2,1)S(1)} %pad_maximum_fusion.1.own_a), channel_id=1, source_target_pairs={{0,2},{1,5},{2,0},{3,7},{4,6},{5,1},{6,4},{7,3},{8,10},{9,13},{10,... | collective-permute-start | bytes 2359304 | tf_op jit(solution)/shard_map/ppermute | solution.py:726
  254.1 1.8 collective-permute-start.17
  254.2 15.3 %collective-permute-start.15 = (bf16[192,1152]{1,0:T(8,128)(2,1)S(1)}, bf16[192,1152]{1,0:T(8,128)(2,1)S(1)}, u32[]{:S(2)}, u32[]{:S(2)}) collective-permute-start(bf16[192,1152]{1,0:T(8,128)(2,1)S(1)} %pad_maximum_fusion.2.own_b), channel_id=1, source_target_pairs={{0,2},{1,5},{2,0},{3,7},{4,6},{5,1},{6,4},{7,3},{8,10},{9,13},{10,... | collective-permute-start | bytes 1327112 | tf_op jit(solution)/shard_map/ppermute | solution.py:726
  269.5 2.9 %collective-permute-start.18 = (bf16[192,2048]{1,0:T(8,128)(2,1)S(1)}, bf16[192,2048]{1,0:T(8,128)(2,1)S(1)}, u32[]{:S(2)}, u32[]{:S(2)}) collective-permute-start(bf16[192,2048]{1,0:T(8,128)(2,1)S(1)} %collective-permute-done.14.own_a), channel_id=1, source_target_pairs={{0,1},{1,0},{2,3},{3,2},{4,5},{5,4},{6,7},{7,6},{8,9},{9,8},{10,11... | collective-permute-start | bytes 2359304 | tf_op jit(solution)/shard_map/ppermute | solution.py:726
  269.5 2.9 %collective-permute-start.19 = (bf16[192,1152]{1,0:T(8,128)(2,1)S(1)}, bf16[192,1152]{1,0:T(8,128)(2,1)S(1)}, u32[]{:S(2)}, u32[]{:S(2)}) collective-permute-start(bf16[192,1152]{1,0:T(8,128)(2,1)S(1)} %collective-permute-done.15.own_b), channel_id=1, source_target_pairs={{0,1},{1,0},{2,3},{3,2},{4,5},{5,4},{6,7},{7,6},{8,9},{9,8},{10,11... | collective-permute-start | bytes 1327112 | tf_op jit(solution)/shard_map/ppermute | solution.py:726

commit v2 on v1

--- a/solution.py
+++ b/solution.py
@@ -878,16 +878,16 @@
     return lax.all_to_all(rows, AXES, split_axis=0, concat_axis=0, tiled=True)
 
 
-def sum_small(parts, n_dev):
+def pack_small(parts):
     flat = jnp.concatenate([part.reshape(-1) for part in parts])
-    size = flat.shape[0]
-    lines = -(-size // 1024) * 8
-    block = jnp.pad(flat, (0, lines * 128 - size)).reshape(1, lines, 128)
-    sent = jnp.broadcast_to(block, (n_dev, lines, 128))
-    total = jnp.sum(exchange(sent), axis=0).reshape(-1)
-    found, start = [], 0
+    lines = -(-flat.shape[0] // 1024) * 8
+    return jnp.pad(flat, (0, lines * 128 - flat.shape[0])).reshape(lines, 128)
+
+
+def unpack_small(packed, parts):
+    flat, found, start = packed.reshape(-1), [], 0
     for part in parts:
-        found.append(total[start : start + part.size].reshape(part.shape))
+        found.append(flat[start : start + part.size].reshape(part.shape))
         start += part.size
     return found
 
@@ -972,31 +972,42 @@
     got_b, sent_a = tie(got_b, sent_a)
     got_a = ring.swap(sent_a, ring.plane[0])
     sent_b, kept_b = step(kept_b, got_b, ring.plane[0])
-    sent_b, grads, dscores = tie(sent_b, grads, dscores)
+    sent_b, dscores = tie(sent_b, dscores)
     got_b = ring.swap(sent_b, ring.plane[0])
-    grad_tokens, attn_gain_rows = tokens_back(grads, weights_t, tokens, attn_gain, dmid)
     grad_table = table_back(dscores, bucket_ids, n_buckets)
-    got_a, got_b, grad_tokens, attn_gain_rows, grad_table, res_rows = tie(
-        got_a, got_b, grad_tokens, attn_gain_rows, grad_table, res_rows
-    )
+    grad_table, res_rows = tie(grad_table, res_rows)
+    layer_out = leave(res_rows, col, middle)
+    got_a, got_b, grad_table, layer_out = tie(got_a, got_b, grad_table, layer_out)
     for shifts in ring.plane[1:] + [ring.near]:
         sent_a, kept_a = step(kept_a, got_a, shifts)
         sent_b, kept_b = step(kept_b, got_b, shifts)
         got_a, got_b = ring.swap(sent_a, shifts), ring.swap(sent_b, shifts)
     value_a, value_b = add(kept_a, got_a), add(kept_b, got_b)
-    value_a, value_b, grad_table, res_rows = tie(value_a, value_b, grad_table, res_rows)
+    value_a, value_b, grads = tie(value_a, value_b, grads)
     got_a, got_b = ring.swap(value_a, ring.far), ring.swap(value_b, ring.far)
-    smalls = sum_small(
-        (attn_gain_rows[0], grad_table, moe_gain_rows[0], grad_router_bias), n_grp * n_loc
-    )
-    layer_out = leave(res_rows, col, middle)
-    got_a, got_b, layer_out = tie(got_a, got_b, layer_out)
+    grad_tokens, attn_gain_rows = tokens_back(grads, weights_t, tokens, attn_gain, dmid)
+    got_a, got_b, grad_tokens, attn_gain_rows = tie(got_a, got_b, grad_tokens, attn_gain_rows)
+    small_parts = (attn_gain_rows[0], grad_table, moe_gain_rows[0], grad_router_bias)
+    small = pack_small(small_parts)
+
+    def swaps(value, todo):
+        for shifts in todo:
+            value = value + ring.swap(value, shifts)
+        return value
+
     value_a, value_b = add(value_a, got_a), add(value_b, got_b)
-    for shifts in reversed(ring.plane[1:] + [ring.near]):
+    turn = list(reversed(ring.plane[1:] + [ring.near]))
+    for place, shifts in enumerate(turn):
         got_a, got_b = ring.swap(value_a, shifts), ring.swap(value_b, shifts)
+        if place == 0:
+            small = swaps(small, ring.plane)
+        if place == len(turn) - 1:
+            small = swaps(small, [ring.near, ring.far])
+        got_a, small = tie(got_a, small)
         value_a = ring.join(value_a, got_a, rank, shifts)
         value_b = ring.join(value_b, got_b, rank, shifts)
-    value_a, value_b, *smalls = tie(value_a, value_b, *smalls)
+    small = swaps(small, [ring.core])
+    smalls = unpack_small(small, small_parts)
     near_a, near_b = ring.swap(value_a, ring.plane[0]), ring.swap(value_b, ring.plane[0])
     core_a, core_b = ring.swap(value_a, ring.core), ring.swap(value_b, ring.core)
     outs = unpack(where, value_a, core_a, value_b, core_b, False, (), width, n_experts)

time: 277 us -> 278 us (level)
  starting transfers between devices: 50.6 us -> 47.2 us
    all_to_all x7 -> x6, starting transfers between devices: 32.4 us -> 27 us  [exchange(): return lax.all_to_all(rows, AXES, split_axis=0, concat_axis=0, tiled=True)]
    ppermute x20 -> x25, starting transfers between devices: 18.2 us -> 20.2 us  [swap(): return lax.ppermute(value, AXES, pairs)]
    ppermute x20 -> x25, waiting for transfers between devices: 38.3 us -> 40.1 us  [swap(): return lax.ppermute(value, AXES, pairs)]
    all_to_all x7 -> x6, waiting for transfers between devices: 30.6 us -> 30.6 us  [exchange(): return lax.all_to_all(rows, AXES, split_axis=0, concat_axis=0, tiled=True)]
  transfers between devices with their start and end apart: 27 -> 31, of which waited for: 16 -> 20; matrix products, arithmetic and copies ran while one was open for 6% -> 6% of each run, Pallas kernels for 47% -> 47%
where the time goes in v2:
time: 278 us; the launch traced here: 276 us
  Pallas kernels  136 us (49%)
  waiting for transfers between devices  70.7 us (25%)
  starting transfers between devices  47.2 us (17%)
  other arithmetic  12 us (4%)
  local copies, waits for them, and re-layouts  8.9 us (3%)
    ppermute x25, waiting for transfers between devices, swap(): return lax.ppermute(value, AXES, pairs)  40.1 us
    pallas_call x2, Pallas kernels, expert(): pl.pallas_call(functools.partial(expert_kernel, n_in=len(earlier)), grid=...  36 us
    all_to_all x6, waiting for transfers between devices, exchange(): return lax.all_to_all(rows, AXES, split_axis=0, concat_axis=0, tiled=True)  30.6 us
    all_to_all x6, starting transfers between devices, exchange(): return lax.all_to_all(rows, AXES, split_axis=0, concat_axis=0, tiled=True)  27 us
    pallas_call x1, Pallas kernels, attend(): pl.pallas_call(functools.partial(attend_kernel, scaling=(width // n_heads...  26.2 us
    pallas_call x1, Pallas kernels, back(): pl.pallas_call(functools.partial(back_kernel, scaling=(width // n_heads)...  20.4 us
    ppermute x25, starting transfers between devices, swap(): return lax.ppermute(value, AXES, pairs)  20.2 us
    pallas_call x1, Pallas kernels, weights_back(): pl.pallas_call(weights_kernel, grid=(ff // block,), in_specs=[whole(n, wi...  16.8 us
  transfers between devices with their start and end apart: 31, of which 20 were waited for; matrix products, arithmetic and copies ran while one was open for 6% of the time, Pallas kernels for 47%

profile of v2, /device:TPU:0, one launch (start us, length us, event | category | flops | bytes accessed | tf_op | source)
XLA Modules:
  0.0 275.9 jit_solution(17545995674775202388)
XLA Ops:
  0.6 3.8 %dispatch.1 = (bf16[1024,768]{1,0:T(8,128)(2,1)}, s32[8,512]{1,0:T(8,128)}, s32[512,128]{1,0:T(8,128)}) custom-call(s32[1,512]{1,0:T(1,128)} %bitcast.127, bf16[512,768]{1,0:T(8,128)(2,1)} %dy_hbm.1), custom_call_target="tpu_custom_call" | custom-call | flops 805306368 | bytes 3145728 | tf_op jit(solution)/shard_map/dispatch/pallas_call | solution.py:79
  4.5 7.3 %all-to-all-start = ((bf16[32,32,768]{2,1,0:T(8,128)(2,1)}), bf16[32,32,768]{2,1,0:T(8,128)(2,1)S(1)}, u32[]{:S(2)}, u32[]{:S(2)}) async-start(bf16[32,32,768]{2,1,0:T(8,128)(2,1)} %bitcast.101), calls=%async_computation | async-start | bytes 3145728 | tf_op jit(solution)/shard_map/all_to_all | solution.py:878
  13.6 26.2 %attend.1 = (bf16[512,768]{1,0:T(8,128)(2,1)}, bf16[512,768]{1,0:T(8,128)(2,1)}, bf16[512,768]{1,0:T(8,128)(2,1)}, bf16[12,512,512]{2,1,0:T(8,128)(2,1)}, bf16[7...) custom-call(bf16[512,768]{1,0:T(8,128)(2,1)} %tok_ref.3, ...), custom_call_target="tpu_custom_call" | custom-call | flops 4831838208 | bytes 15728640 | tf_op jit(solution)/shard_map/attend/pallas_call | solution.py:179
  39.8 9.5 %all-to-all-done = bf16[32,32,768]{2,1,0:T(8,128)(2,1)S(1)} async-done(((bf16[32,32,768]{2,1,0:T(8,128)(2,1)}), bf16[32,32,768]{2,1,0:T(8,128)(2,1)S(1)}, u32[]{:S(2)}, u32[]{:S(2)}) %all-to-all-start) | async-done | bytes 1572896 | tf_op jit(solution)/shard_map/all_to_all | solution.py:878
  49.3 3.7 %all-to-all-start.1 = ((bf16[32,16,768]{2,1,0:T(8,128)(2,1)}), bf16[32,16,768]{2,1,0:T(8,128)(2,1)S(1)}, u32[]{:S(2)}, u32[]{:S(2)}) async-start(bf16[32,16,768]{2,1,0:T(8,128)(2,1)} %bitcast.113), calls=%async_computation.1 | async-start | bytes 1572864 | tf_op jit(solution)/shard_map/all_to_all | solution.py:878
  53.0 5.2 %arrive.1 = (bf16[512,768]{1,0:T(8,128)(2,1)}, bf16[512,768]{1,0:T(8,128)(2,1)}, f32[512,128]{1,0:T(8,128)}, f32[512,128]{1,0:T(8,128)}) custom-call(bf16[1024,768]{1,0:T(8,128)(2,1)} %bitcast.100), custom_call_target="tpu_custom_call" | custom-call | flops 1610612736 | bytes 3145728 | tf_op jit(solution)/shard_map/arrive/pallas_call | solution.py:263
  58.2 15.4 %all-to-all-done.1 = bf16[32,16,768]{2,1,0:T(8,128)(2,1)S(1)} async-done(((bf16[32,16,768]{2,1,0:T(8,128)(2,1)}), bf16[32,16,768]{2,1,0:T(8,128)(2,1)S(1)}, u32[]{:S(2)}, u32[]{:S(2)}) %all-to-all-start.1) | async-done | bytes 786464 | tf_op jit(solution)/shard_map/all_to_all | solution.py:878
  73.6 3.8 %all-to-all-start.2 = ((bf16[32,16,768]{2,1,0:T(8,128)(2,1)}), bf16[32,16,768]{2,1,0:T(8,128)(2,1)S(1)}, u32[]{:S(2)}, u32[]{:S(2)}) async-start(bf16[32,16,768]{2,1,0:T(8,128)(2,1)} %bitcast.8), calls=%async_computation.2 | async-start | bytes 1572864 | tf_op jit(solution)/shard_map/all_to_all | solution.py:878
  78.4 18.0 %expert.2 = (bf16[512,768]{1,0:T(8,128)(2,1)}, bf16[512,768]{1,0:T(8,128)(2,1)}, bf16[1024,3072]{1,0:T(8,128)(2,1)}, bf16[1024,3072]{1,0:T(8,128)(2,1)}, bf16[1024,768]{1,0:T(8,128)(2,1)}, /*index=5*/f32[1024,32]{1,0:T(8,128)}) custom-call(s32[1]{0:T(128)} %bitcast.me_ref, bf16[512,768]{1,0:T(8,128)(2,1)} %bitcast.108, ...), custom_call_target="tpu_custom_call" | custom-call | flops 9663676416 | bytes 37748736 | tf_op jit(solution)/shard_map/expert/pallas_call | solution.py:338
  96.3 1.5 all-to-all-done.2
  97.9 4.2 %all-to-all-start.3 = ((bf16[32,16,768]{2,1,0:T(8,128)(2,1)}), bf16[32,16,768]{2,1,0:T(8,128)(2,1)S(1)}, u32[]{:S(2)}, u32[]{:S(2)}) async-start(bf16[32,16,768]{2,1,0:T(8,128)(2,1)} %bitcast.114), calls=%async_computation.3 | async-start | bytes 1572864 | tf_op jit(solution)/shard_map/all_to_all | solution.py:878
  102.0 18.0 %expert.3 = (bf16[512,768]{1,0:T(8,128)(2,1)}, bf16[512,768]{1,0:T(8,128)(2,1)}, bf16[1024,3072]{1,0:T(8,128)(2,1)}, bf16[1024,3072]{1,0:T(8,128)(2,1)}, bf16[1024,768]{1,0:T(8,128)(2,1)}, /*index=5*/f32[1024,32]{1,0:T(8,128)}) custom-call(s32[1]{0:T(128)} %bitcast.me_ref, ...), custom_call_target="tpu_custom_call", output_to_operand_aliasing={{2}: (8, {}), {3}: (9, {}), {4}: (10, {}), {5}: (11, {})} | custom-call | flops 9663676416 | bytes 37748736 | tf_op jit(solution)/shard_map/expert/pallas_call | solution.py:338
  120.1 2.6 all-to-all-done.3
  122.6 3.6 %all-to-all-start.4 = ((bf16[32,16,768]{2,1,0:T(8,128)(2,1)}), bf16[32,16,768]{2,1,0:T(8,128)(2,1)S(1)}, u32[]{:S(2)}, u32[]{:S(2)}) async-start(bf16[32,16,768]{2,1,0:T(8,128)(2,1)} %bitcast.112), calls=%async_computation.4 | async-start | bytes 1572864 | tf_op jit(solution)/shard_map/all_to_all | solution.py:878
  126.4 1.4 pad_maximum_fusion
  127.7 16.8 %weights_back.1 = (f32[768,3072]{1,0:T(8,128)}, f32[3072,768]{1,0:T(8,128)}, f32[768,128]{1,0:T(8,128)}, f32[8,32]{1,0:T(8,128)}) custom-call(bf16[512,768]{1,0:T(8,128)(2,1)} %bitcast.109, bf16[512,768]{1,0:T(8,128)(2,1)} %bitcast.111, bf16[1024,3072]{1,0:T(8,128)(2,1)} %get-tuple-element.177.hid_ref, bf16[1024,3072]{1,0:T(8,128)(2,1)} %get-tuple-element.178.dpre_ref, ...), custom_call_target="tpu_custom_call" | custom-call | flops 9663676416 | bytes 18874368 | tf_op jit(solution)/shard_map/weights_back/pallas_call | solution.py:409
  145.3 1.6 all-to-all-done.4
  147.8 4.4 %all-to-all-start.5 = ((bf16[32,32,768]{2,1,0:T(8,128)(2,1)}), bf16[32,32,768]{2,1,0:T(8,128)(2,1)S(1)}, u32[]{:S(2)}, u32[]{:S(2)}) async-start(bf16[32,32,768]{2,1,0:T(8,128)(2,1)} %bitcast.27), calls=%async_computation.5 | async-start | bytes 3145728 | tf_op jit(solution)/shard_map/all_to_all | solution.py:878
  152.3 20.4 %back.1 = (f32[512,768]{1,0:T(8,128)}, bf16[384,2048]{1,0:T(8,128)(2,1)}, bf16[384,2048]{1,0:T(8,128)(2,1)}, f32[8,768]{1,0:T(8,128)}, bf16[512,2304]{1,0:T(8,12...) custom-call(s32[1]{0:T(128)S(6)} %and.16.core_ref, ...), custom_call_target="tpu_custom_call" | custom-call | flops 1000 | bytes 1000 | tf_op jit(solution)/shard_map/back/pallas_call | solution.py:619
  173.3 4.4 %collective-permute-done.1 = bf16[384,2048]{1,0:T(8,128)(2,1)S(1)} collective-permute-done((bf16[384,2048]{1,0:T(8,128)(2,1)}, bf16[384,2048]{1,0:T(8,128)(2,1)S(1)}, u32[]{:S(2)}, u32[]{:S(2)}) %collective-permute-start.1) | collective-permute-done | bytes 1572896 | tf_op jit(solution)/shard_map/ppermute | solution.py:726
  177.7 2.8 %fusion = bf16[192,2048]{1,0:T(8,128)(2,1)} fusion(bf16[2,192,2048]{2,1,0:T(8,128)(2,1)S(1)} %bitcast.98, s32[]{:T(128)S(6)} %select_n.129, bf16[2,192,2048]{2,1,0:T(8,128)(2,1)} %bitcast.96), kind=kLoop, calls=%fused_computation.5 | loop fusion | flops 1572864 | bytes 2359300 | tf_op jit(solution)/shard_map/convert_element_type | solution.py:705
  180.5 2.1 fusion.1
  184.6 1.1 add_convert_fusion.2
  185.8 1.4 add_convert_fusion
  187.2 10.0 %table_back.1 = f32[12,32]{1,0:T(8,128)} custom-call(bf16[12,512,512]{2,1,0:T(8,128)(2,1)} %get-tuple-element.205.ds_ref, s32[512,512]{1,0:T(8,128)} %bucket_ref.3), custom_call_target="tpu_custom_call" | custom-call | flops 3221225472 | bytes 6291456 | tf_op jit(solution)/shard_map/table_back/pallas_call | solution.py:688
  197.2 1.1 copy-done
  198.3 4.0 %leave.1 = bf16[512,768]{1,0:T(8,128)(2,1)} custom-call(bf16[1024,768]{1,0:T(8,128)(2,1)} %bitcast.89, s32[512,128]{1,0:T(8,128)} %get-tuple-element.186.col_hbm.col_ref, f32[512,768]{1,0:T(8,128)} %get-tuple-element.187.mid_hbm.mid_ref), custom_call_target="tpu_custom_call" | custom-call | flops 805306368 | bytes 3932160 | tf_op jit(solution)/shard_map/leave/pallas_call | solution.py:868
  202.3 1.2 collective-permute-start.6
  205.7 1.1 add_convert_fusion.4
  206.8 1.5 collective-permute-done.6
  209.5 3.1 %collective-permute-done.4 = bf16[96,2048]{1,0:T(8,128)(2,1)S(1)} collective-permute-done((bf16[96,2048]{1,0:T(8,128)(2,1)S(1)}, bf16[96,2048]{1,0:T(8,128)(2,1)S(1)}, u32[]{:S(2)}, u32[]{:S(2)}) %collective-permute-start.4) | collective-permute-done | bytes 393248 | tf_op jit(solution)/shard_map/ppermute | solution.py:726
  212.6 1.4 collective-permute-start.5
  214.0 4.3 %collective-permute-done.5 = bf16[48,2048]{1,0:T(8,128)(2,1)S(1)} collective-permute-done((bf16[48,2048]{1,0:T(8,128)(2,1)S(1)}, bf16[48,2048]{1,0:T(8,128)(2,1)S(1)}, u32[]{:S(2)}, u32[]{:S(2)}) %collective-permute-start.5) | collective-permute-done | bytes 196640 | tf_op jit(solution)/shard_map/ppermute | solution.py:726
  218.4 2.1 collective-permute-start.8
  222.3 7.2 %tokens_back.1 = (bf16[512,768]{1,0:T(8,128)(2,1)}, f32[8,768]{1,0:T(8,128)}) custom-call(bf16[512,2304]{1,0:T(8,128)(2,1)} %get-tuple-element.231.grads_ref, bf16[2304,768]{1,0:T(8,128)(2,1)} %get-tuple-element.232.wt_ref, bf16[512,768]{1,0:T(8,128)(2,1)} %tok_ref.3, f32[1,768]{1,0:T(1,128)} %reshape.226.gain_ref, f32[512,768]{1,0:T(8,128)} %get-tuple-element.233.dmid_ref), custom_call_target="tpu_custom_call" | custom-call | flops 1811939328 | bytes 9043968 | tf_op jit(solution)/shard_map/tokens_back/pallas_call | solution.py:840
  229.5 3.3 %collective-permute-done.9 = bf16[48,1152]{1,0:T(8,128)(2,1)S(1)} collective-permute-done((bf16[48,1152]{1,0:T(8,128)(2,1)S(1)}, bf16[48,1152]{1,0:T(8,128)(2,1)S(1)}, u32[]{:S(2)}, u32[]{:S(2)}) %collective-permute-start.9) | collective-permute-done | bytes 110624 | tf_op jit(solution)/shard_map/ppermute | solution.py:726
  235.2 2.0 collective-permute-done.11
  237.2 1.2 collective-permute-start.12
  238.8 2.1 collective-permute-done.12
  241.7 1.2 collective-permute-start.14
  243.3 2.0 collective-permute-done.14
  245.3 2.6 collective-permute-start.15
  248.6 1.3 collective-permute-done.15
  251.7 2.3 collective-permute-done.18
  256.0 3.1 %unpack.2 = (f32[768,768]{1,0:T(8,128)}, f32[768,768]{1,0:T(8,128)}, f32[768,768]{1,0:T(8,128)}, f32[768,768]{1,0:T(8,128)}, f32[32,768]{1,0:T(8,128)S(1)}) custom-call(s32[3]{0:T(128)S(1)} %pad_add_fusion.where_ref, bf16[192,2048]{1,0:T(8,128)(2,1)S(1)} %pad_maximum_fusion.1.own_a, bf16[192,2048]{1,0:T(8,128)(2,1)S(1)} %collective-permute-done.20.core_a, ...), custom_call_target="tpu_custom_call" | custom-call | flops 147456 | bytes 3538944 | tf_op jit(solution)/shard_map/unpack/pallas_call | solution.py:791
  259.1 8.8 %collective-permute-done.19.own_b = bf16[192,1152]{1,0:T(8,128)(2,1)S(1)} collective-permute-done((bf16[192,1152]{1,0:T(8,128)(2,1)S(1)}, bf16[192,1152]{1,0:T(8,128)(2,1)S(1)}, u32[]{:S(2)}, u32[]{:S(2)}) %collective-permute-start.19) | collective-permute-done | bytes 442400 | tf_op jit(solution)/shard_map/ppermute | solution.py:726
  268.4 2.4 collective-permute-done.24
  272.6 3.3 %unpack.3 = (f32[768,768]{1,0:T(8,128)}, f32[768,768]{1,0:T(8,128)}, f32[768,768]{1,0:T(8,128)}, f32[768,768]{1,0:T(8,128)}, f32[32,768]{1,0:T(8,128)}) custom-call(s32[3]{0:T(128)S(1)} %pad_add_fusion.where_ref, bf16[192,2048]{1,0:T(8,128)(2,1)S(1)} %collective-permute-done.16.own_a, ...), custom_call_target="tpu_custom_call", output_to_operand_aliasing={{0}: (6, {}), {1}: (7, {}), {2}: (8, {}), {3}: (9, {})} | custom-call | flops 147456 | bytes 3538944 | tf_op jit(solution)/shard_map/unpack/pallas_call | solution.py:791
  (101 shorter events, 23.0 us)
Async XLA Ops:
  4.5 7.3 %copy-start.14 = (f32[768]{0:T(1024)S(1)}, f32[768]{0:T(1024)}, u32[]{:S(2)}) copy-start(f32[768]{0:T(1024)} %param.21) | copy-start | bytes 9220
  4.5 7.9 %copy-start.15 = (f32[768]{0:T(1024)S(1)}, f32[768]{0:T(1024)}, u32[]{:S(2)}) copy-start(f32[768]{0:T(1024)} %param.23) | copy-start | bytes 9220
  4.5 8.5 %copy-start.13 = (f32[32,12]{0,1:T(8,128)S(1)}, f32[32,12]{0,1:T(8,128)}, u32[]{:S(2)}) copy-start(f32[32,12]{0,1:T(8,128)} %param.22) | copy-start | bytes 4612
  4.5 44.8 %all-to-all-start = ((bf16[32,32,768]{2,1,0:T(8,128)(2,1)}), bf16[32,32,768]{2,1,0:T(8,128)(2,1)S(1)}, u32[]{:S(2)}, u32[]{:S(2)}) async-start(bf16[32,32,768]{2,1,0:T(8,128)(2,1)} %bitcast.101), calls=%async_computation | async-start | bytes 3145728 | tf_op jit(solution)/shard_map/all_to_all | solution.py:878
  49.3 3.7 %copy-start.5 = (bf16[32,32,768]{2,1,0:T(8,128)(2,1)}, bf16[32,32,768]{2,1,0:T(8,128)(2,1)S(1)}, u32[]{:S(2)}) copy-start(bf16[32,32,768]{2,1,0:T(8,128)(2,1)S(1)} %all-to-all-done) | copy-start | bytes 4718596
  49.3 24.3 %all-to-all-start.1 = ((bf16[32,16,768]{2,1,0:T(8,128)(2,1)}), bf16[32,16,768]{2,1,0:T(8,128)(2,1)S(1)}, u32[]{:S(2)}, u32[]{:S(2)}) async-start(bf16[32,16,768]{2,1,0:T(8,128)(2,1)} %bitcast.113), calls=%async_computation.1 | async-start | bytes 1572864 | tf_op jit(solution)/shard_map/all_to_all | solution.py:878
  58.2 19.2 %copy-start.11 = (f32[768,32]{0,1:T(8,128)S(1)}, f32[768,32]{0,1:T(8,128)}, u32[]{:S(2)}) copy-start(f32[768,32]{0,1:T(8,128)} %param.24) | copy-start | bytes 294916
  73.6 4.8 %copy-start.7 = (bf16[32,16,768]{2,1,0:T(8,128)(2,1)}, bf16[32,16,768]{2,1,0:T(8,128)(2,1)S(1)}, u32[]{:S(2)}) copy-start(bf16[32,16,768]{2,1,0:T(8,128)(2,1)S(1)} %all-to-all-done.1) | copy-start | bytes 2359300
  73.6 24.2 %all-to-all-start.2 = ((bf16[32,16,768]{2,1,0:T(8,128)(2,1)}), bf16[32,16,768]{2,1,0:T(8,128)(2,1)S(1)}, u32[]{:S(2)}, u32[]{:S(2)}) async-start(bf16[32,16,768]{2,1,0:T(8,128)(2,1)} %bitcast.8), calls=%async_computation.2 | async-start | bytes 1572864 | tf_op jit(solution)/shard_map/all_to_all | solution.py:878
  97.9 4.2 %copy-start.8 = (bf16[32,16,768]{2,1,0:T(8,128)(2,1)}, bf16[32,16,768]{2,1,0:T(8,128)(2,1)S(1)}, u32[]{:S(2)}) copy-start(bf16[32,16,768]{2,1,0:T(8,128)(2,1)S(1)} %all-to-all-done.2) | copy-start | bytes 2359300
  97.9 24.8 %all-to-all-start.3 = ((bf16[32,16,768]{2,1,0:T(8,128)(2,1)}), bf16[32,16,768]{2,1,0:T(8,128)(2,1)S(1)}, u32[]{:S(2)}, u32[]{:S(2)}) async-start(bf16[32,16,768]{2,1,0:T(8,128)(2,1)} %bitcast.114), calls=%async_computation.3 | async-start | bytes 1572864 | tf_op jit(solution)/shard_map/all_to_all | solution.py:878
  120.0 6.3 %copy-start.9 = (bf16[512,768]{1,0:T(8,128)(2,1)S(1)}, bf16[512,768]{1,0:T(8,128)(2,1)}, u32[]{:S(2)}) copy-start(bf16[512,768]{1,0:T(8,128)(2,1)} %get-tuple-element.175) | copy-start | bytes 2359300
  120.1 6.3 %copy-start.10 = (bf16[512,768]{1,0:T(8,128)(2,1)S(1)}, bf16[512,768]{1,0:T(8,128)(2,1)}, u32[]{:S(2)}) copy-start(bf16[512,768]{1,0:T(8,128)(2,1)} %get-tuple-element.176) | copy-start | bytes 2359300
  122.6 5.1 %copy-start.1 = (bf16[32,16,768]{2,1,0:T(8,128)(2,1)}, bf16[32,16,768]{2,1,0:T(8,128)(2,1)S(1)}, u32[]{:S(2)}) copy-start(bf16[32,16,768]{2,1,0:T(8,128)(2,1)S(1)} %all-to-all-done.3) | copy-start | bytes 2359300
  122.6 24.2 %all-to-all-start.4 = ((bf16[32,16,768]{2,1,0:T(8,128)(2,1)}), bf16[32,16,768]{2,1,0:T(8,128)(2,1)S(1)}, u32[]{:S(2)}, u32[]{:S(2)}) async-start(bf16[32,16,768]{2,1,0:T(8,128)(2,1)} %bitcast.112), calls=%async_computation.4 | async-start | bytes 1572864 | tf_op jit(solution)/shard_map/all_to_all | solution.py:878
  146.9 0.9 copy-start.2
  147.8 49.3 %all-to-all-start.5 = ((bf16[32,32,768]{2,1,0:T(8,128)(2,1)}), bf16[32,32,768]{2,1,0:T(8,128)(2,1)S(1)}, u32[]{:S(2)}, u32[]{:S(2)}) async-start(bf16[32,32,768]{2,1,0:T(8,128)(2,1)} %bitcast.27), calls=%async_computation.5 | async-start | bytes 3145728 | tf_op jit(solution)/shard_map/all_to_all | solution.py:878
  172.7 5.0 %collective-permute-start.1 = (bf16[384,2048]{1,0:T(8,128)(2,1)}, bf16[384,2048]{1,0:T(8,128)(2,1)S(1)}, u32[]{:S(2)}, u32[]{:S(2)}) collective-permute-start(bf16[384,2048]{1,0:T(8,128)(2,1)} %get-tuple-element.197), channel_id=1, source_target_pairs={{0,1},{1,0},{2,3},{3,2},{4,5},{5,4},{6,7},{7,6},{8,9},{9,8},{10,11... | collective-permute-start | bytes 4718600 | tf_op jit(solution)/shard_map/ppermute | solution.py:726
  172.8 7.7 %collective-permute-start = (bf16[384,1152]{1,0:T(8,128)(2,1)}, bf16[384,1152]{1,0:T(8,128)(2,1)}, u32[]{:S(2)}, u32[]{:S(2)}) collective-permute-start(bf16[384,1152]{1,0:T(8,128)(2,1)} %get-tuple-element.195), channel_id=1, source_target_pairs={{0,1},{1,0},{2,3},{3,2},{4,5},{5,4},{6,7},{7,6},{8,9},{9,8},{10,11... | collective-permute-start | bytes 2654216 | tf_op jit(solution)/shard_map/ppermute | solution.py:726
  173.3 7.2 %copy-start.6 = (bf16[384,1152]{1,0:T(8,128)(2,1)S(1)}, bf16[384,1152]{1,0:T(8,128)(2,1)}, u32[]{:S(2)}) copy-start(bf16[384,1152]{1,0:T(8,128)(2,1)} %get-tuple-element.219) | copy-start | bytes 2654212
  177.7 4.9 %copy-start.4 = (bf16[384,2048]{1,0:T(8,128)(2,1)}, bf16[384,2048]{1,0:T(8,128)(2,1)S(1)}, u32[]{:S(2)}) copy-start(bf16[384,2048]{1,0:T(8,128)(2,1)S(1)} %collective-permute-done.1) | copy-start | bytes 4718596
  180.5 5.2 %copy-start.3 = (bf16[384,2048]{1,0:T(8,128)(2,1)S(1)}, bf16[384,2048]{1,0:T(8,128)(2,1)}, u32[]{:S(2)}) copy-start(bf16[384,2048]{1,0:T(8,128)(2,1)} %get-tuple-element.210) | copy-start | bytes 4718596
  182.6 19.7 %collective-permute-start.3 = (bf16[192,1152]{1,0:T(8,128)(2,1)}, bf16[192,1152]{1,0:T(8,128)(2,1)S(1)}, u32[]{:S(2)}, u32[]{:S(2)}) collective-permute-start(bf16[192,1152]{1,0:T(8,128)(2,1)} %fusion.1), channel_id=1, source_target_pairs={{0,2},{1,5},{2,0},{3,7},{4,6},{5,1},{6,4},{7,3},{8,10},{9,13},{10,... | collective-permute-start | bytes 1327112 | tf_op jit(solution)/shard_map/ppermute | solution.py:726
  183.6 18.7 %collective-permute-start.2 = (bf16[192,2048]{1,0:T(8,128)(2,1)}, bf16[192,2048]{1,0:T(8,128)(2,1)}, u32[]{:S(2)}, u32[]{:S(2)}) collective-permute-start(bf16[192,2048]{1,0:T(8,128)(2,1)} %fusion), channel_id=1, source_target_pairs={{0,2},{1,5},{2,0},{3,7},{4,6},{5,1},{6,4},{7,3},{8,10},{9,13},{10,... | collective-permute-start | bytes 2359304 | tf_op jit(solution)/shard_map/ppermute | solution.py:726
  197.2 1.1 copy-start
  202.3 6.0 %collective-permute-start.6 = (bf16[96,1152]{1,0:T(8,128)(2,1)S(1)}, bf16[96,1152]{1,0:T(8,128)(2,1)S(1)}, u32[]{:S(2)}, u32[]{:S(2)}) collective-permute-start(bf16[96,1152]{1,0:T(8,128)(2,1)S(1)} %fusion.4), channel_id=1, source_target_pairs={{0,4},{1,3},{2,6},{3,1},{4,0},{5,7},{6,2},{7,5},{8,12},{9,11},{10,... | collective-permute-start | bytes 663560 | tf_op jit(solution)/shard_map/ppermute | solution.py:726
  204.7 7.9 %collective-permute-start.4 = (bf16[96,2048]{1,0:T(8,128)(2,1)S(1)}, bf16[96,2048]{1,0:T(8,128)(2,1)S(1)}, u32[]{:S(2)}, u32[]{:S(2)}) collective-permute-start(bf16[96,2048]{1,0:T(8,128)(2,1)S(1)} %fusion.2), channel_id=1, source_target_pairs={{0,4},{1,3},{2,6},{3,1},{4,0},{5,7},{6,2},{7,5},{8,12},{9,11},{10,... | collective-permute-start | bytes 1179656 | tf_op jit(solution)/shard_map/ppermute | solution.py:726
  205.7 15.6 %copy-start.12 = (f32[12,32]{1,0:T(8,128)S(1)}, f32[12,32]{1,0:T(8,128)}, u32[]{:S(2)}) copy-start(f32[12,32]{1,0:T(8,128)} %table_back.1) | copy-start | bytes 4612
  208.4 5.6 %collective-permute-start.7 = (bf16[48,1152]{1,0:T(8,128)(2,1)S(1)}, bf16[48,1152]{1,0:T(8,128)(2,1)S(1)}, u32[]{:S(2)}, u32[]{:S(2)}) collective-permute-start(bf16[48,1152]{1,0:T(8,128)(2,1)S(1)} %fusion.8), channel_id=1, source_target_pairs={{0,8},{1,9},{2,10},{3,11},{4,12},{5,13},{6,14},{7,15},{8,0},{9,1},... | collective-permute-start | bytes 331784 | tf_op jit(solution)/shard_map/ppermute | solution.py:726
  212.6 5.7 %collective-permute-start.5 = (bf16[48,2048]{1,0:T(8,128)(2,1)S(1)}, bf16[48,2048]{1,0:T(8,128)(2,1)S(1)}, u32[]{:S(2)}, u32[]{:S(2)}) collective-permute-start(bf16[48,2048]{1,0:T(8,128)(2,1)S(1)} %fusion.6), channel_id=1, source_target_pairs={{0,8},{1,9},{2,10},{3,11},{4,12},{5,13},{6,14},{7,15},{8,0},{9,1},... | collective-permute-start | bytes 589832 | tf_op jit(solution)/shard_map/ppermute | solution.py:726
  218.4 14.3 %collective-permute-start.8 = (bf16[48,2048]{1,0:T(8,128)(2,1)S(1)}, bf16[48,2048]{1,0:T(8,128)(2,1)S(1)}, u32[]{:S(2)}, u32[]{:S(2)}) collective-permute-start(bf16[48,2048]{1,0:T(8,128)(2,1)S(1)} %fusion.3), channel_id=1, source_target_pairs={{0,16},{1,17},{2,18},{3,19},{4,20},{5,21},{6,22},{7,23},{8,24},{9,... | collective-permute-start | bytes 589832 | tf_op jit(solution)/shard_map/ppermute | solution.py:726
  221.4 11.3 %collective-permute-start.9 = (bf16[48,1152]{1,0:T(8,128)(2,1)S(1)}, bf16[48,1152]{1,0:T(8,128)(2,1)S(1)}, u32[]{:S(2)}, u32[]{:S(2)}) collective-permute-start(bf16[48,1152]{1,0:T(8,128)(2,1)S(1)} %fusion.5), channel_id=1, source_target_pairs={{0,16},{1,17},{2,18},{3,19},{4,20},{5,21},{6,22},{7,23},{8,24},{9,... | collective-permute-start | bytes 331784 | tf_op jit(solution)/shard_map/ppermute | solution.py:726
  233.5 3.7 %collective-permute-start.11 = (f32[16,128]{1,0:T(8,128)S(1)}, f32[16,128]{1,0:T(8,128)S(1)}, u32[]{:S(2)}, u32[]{:S(2)}) collective-permute-start(f32[16,128]{1,0:T(8,128)S(1)} %fusion.10), channel_id=1, source_target_pairs={{0,2},{1,5},{2,0},{3,7},{4,6},{5,1},{6,4},{7,3},{8,10},{9,13},{10,... | collective-permute-start | bytes 24584 | tf_op jit(solution)/shard_map/ppermute | solution.py:726
  234.7 7.0 %collective-permute-start.10 = (bf16[48,2048]{1,0:T(8,128)(2,1)S(1)}, bf16[48,2048]{1,0:T(8,128)(2,1)S(1)}, u32[]{:S(2)}, u32[]{:S(2)}) collective-permute-start(bf16[48,2048]{1,0:T(8,128)(2,1)S(1)} %add_convert_fusion.8), channel_id=1, source_target_pairs={{0,8},{1,9},{2,10},{3,11},{4,12},{5,13},{6,14},{7,15},{8,0},{9,1},... | collective-permute-start | bytes 589832 | tf_op jit(solution)/shard_map/ppermute | solution.py:726
  237.2 3.7 %collective-permute-start.12 = (f32[16,128]{1,0:T(8,128)S(1)}, f32[16,128]{1,0:T(8,128)S(1)}, u32[]{:S(2)}, u32[]{:S(2)}) collective-permute-start(f32[16,128]{1,0:T(8,128)S(1)} %fusion.11), channel_id=1, source_target_pairs={{0,4},{1,3},{2,6},{3,1},{4,0},{5,7},{6,2},{7,5},{8,12},{9,11},{10,... | collective-permute-start | bytes 24584 | tf_op jit(solution)/shard_map/ppermute | solution.py:726
  238.5 4.8 %collective-permute-start.17 = (bf16[48,1152]{1,0:T(8,128)(2,1)S(1)}, bf16[48,1152]{1,0:T(8,128)(2,1)S(1)}, u32[]{:S(2)}, u32[]{:S(2)}) collective-permute-start(bf16[48,1152]{1,0:T(8,128)(2,1)S(1)} %add_convert_fusion.11), channel_id=1, source_target_pairs={{0,8},{1,9},{2,10},{3,11},{4,12},{5,13},{6,14},{7,15},{8,0},{9,1},... | collective-permute-start | bytes 331784 | tf_op jit(solution)/shard_map/ppermute | solution.py:726
  241.7 3.7 %collective-permute-start.14 = (f32[16,128]{1,0:T(8,128)S(1)}, f32[16,128]{1,0:T(8,128)S(1)}, u32[]{:S(2)}, u32[]{:S(2)}) collective-permute-start(f32[16,128]{1,0:T(8,128)S(1)} %fusion.12), channel_id=1, source_target_pairs={{0,8},{1,9},{2,10},{3,11},{4,12},{5,13},{6,14},{7,15},{8,0},{9,1},... | collective-permute-start | bytes 24584 | tf_op jit(solution)/shard_map/ppermute | solution.py:726
  242.9 7.8 %collective-permute-start.13 = (bf16[96,2048]{1,0:T(8,128)(2,1)S(1)}, bf16[96,2048]{1,0:T(8,128)(2,1)S(1)}, u32[]{:S(2)}, u32[]{:S(2)}) collective-permute-start(bf16[96,2048]{1,0:T(8,128)(2,1)S(1)} %pad_maximum_fusion.3), channel_id=1, source_target_pairs={{0,4},{1,3},{2,6},{3,1},{4,0},{5,7},{6,2},{7,5},{8,12},{9,11},{10,... | collective-permute-start | bytes 1179656 | tf_op jit(solution)/shard_map/ppermute | solution.py:726
  245.3 4.5 %collective-permute-start.15 = (f32[16,128]{1,0:T(8,128)S(1)}, f32[16,128]{1,0:T(8,128)S(1)}, u32[]{:S(2)}, u32[]{:S(2)}) collective-permute-start(f32[16,128]{1,0:T(8,128)S(1)} %add.159), channel_id=1, source_target_pairs={{0,16},{1,17},{2,18},{3,19},{4,20},{5,21},{6,22},{7,23},{8,24},{9,... | collective-permute-start | bytes 24584 | tf_op jit(solution)/shard_map/ppermute | solution.py:726
  248.0 6.0 %collective-permute-start.18 = (bf16[96,1152]{1,0:T(8,128)(2,1)S(1)}, bf16[96,1152]{1,0:T(8,128)(2,1)S(1)}, u32[]{:S(2)}, u32[]{:S(2)}) collective-permute-start(bf16[96,1152]{1,0:T(8,128)(2,1)S(1)} %pad_maximum_fusion.4), channel_id=1, source_target_pairs={{0,4},{1,3},{2,6},{3,1},{4,0},{5,7},{6,2},{7,5},{8,12},{9,11},{10,... | collective-permute-start | bytes 663560 | tf_op jit(solution)/shard_map/ppermute | solution.py:726
  251.0 5.0 %collective-permute-start.20 = (bf16[192,2048]{1,0:T(8,128)(2,1)S(1)}, bf16[192,2048]{1,0:T(8,128)(2,1)S(1)}, u32[]{:S(2)}, u32[]{:S(2)}) collective-permute-start(bf16[192,2048]{1,0:T(8,128)(2,1)S(1)} %pad_maximum_fusion.1.own_a), channel_id=1, source_target_pairs={{0,1},{1,0},{2,3},{3,2},{4,5},{5,4},{6,7},{7,6},{8,9},{9,8},{10,11... | collective-permute-start | bytes 2359304 | tf_op jit(solution)/shard_map/ppermute | solution.py:726
  251.1 16.8 %collective-permute-start.16 = (bf16[192,2048]{1,0:T(8,128)(2,1)S(1)}, bf16[192,2048]{1,0:T(8,128)(2,1)S(1)}, u32[]{:S(2)}, u32[]{:S(2)}) collective-permute-start(bf16[192,2048]{1,0:T(8,128)(2,1)S(1)} %pad_maximum_fusion.1.own_a), channel_id=1, source_target_pairs={{0,2},{1,5},{2,0},{3,7},{4,6},{5,1},{6,4},{7,3},{8,10},{9,13},{10,... | collective-permute-start | bytes 2359304 | tf_op jit(solution)/shard_map/ppermute | solution.py:726
  254.1 1.9 collective-permute-start.21
  254.2 13.7 %collective-permute-start.19 = (bf16[192,1152]{1,0:T(8,128)(2,1)S(1)}, bf16[192,1152]{1,0:T(8,128)(2,1)S(1)}, u32[]{:S(2)}, u32[]{:S(2)}) collective-permute-start(bf16[192,1152]{1,0:T(8,128)(2,1)S(1)} %pad_maximum_fusion.2.own_b), channel_id=1, source_target_pairs={{0,2},{1,5},{2,0},{3,7},{4,6},{5,1},{6,4},{7,3},{8,10},{9,13},{10,... | collective-permute-start | bytes 1327112 | tf_op jit(solution)/shard_map/ppermute | solution.py:726
  267.9 4.7 %collective-permute-start.22 = (bf16[192,2048]{1,0:T(8,128)(2,1)S(1)}, bf16[192,2048]{1,0:T(8,128)(2,1)S(1)}, u32[]{:S(2)}, u32[]{:S(2)}) collective-permute-start(bf16[192,2048]{1,0:T(8,128)(2,1)S(1)} %collective-permute-done.16.own_a), channel_id=1, source_target_pairs={{0,1},{1,0},{2,3},{3,2},{4,5},{5,4},{6,7},{7,6},{8,9},{9,8},{10,11... | collective-permute-start | bytes 2359304 | tf_op jit(solution)/shard_map/ppermute | solution.py:726
  267.9 4.7 %collective-permute-start.23 = (bf16[192,1152]{1,0:T(8,128)(2,1)S(1)}, bf16[192,1152]{1,0:T(8,128)(2,1)S(1)}, u32[]{:S(2)}, u32[]{:S(2)}) collective-permute-start(bf16[192,1152]{1,0:T(8,128)(2,1)S(1)} %collective-permute-done.19.own_b), channel_id=1, source_target_pairs={{0,1},{1,0},{2,3},{3,2},{4,5},{5,4},{6,7},{7,6},{8,9},{9,8},{10,11... | collective-permute-start | bytes 1327112 | tf_op jit(solution)/shard_map/ppermute | solution.py:726
  268.4 2.4 collective-permute-start.24
